TPU v7x, 128 devices: a whole 4x4x4 slice. The times are simulated.
128 devices in a mesh: expert: 16 (over x, z), shard: 8 (over y, core).
Axes of the slice: x: 4, y: 4, z: 4, core: 2. Of those that a mesh axis runs over, the one named last changes fastest.
Arguments:
- hidden_in: bfloat16 [16384, 2048], P(('expert', 'shard')), may hold values from -6 to 6
- cotangent: bfloat16 [16384, 2048], P(('expert', 'shard')), may hold values from -6 to 6
- lengths: int32 [16, 3], P('expert'), may hold values from 1 to 768, 1024 in all within a row
- dealing: int32 [16, 1024], P('expert'), may hold values from 0 to 1023, each once within a row
- routes: int32 [16384, 2], P(('expert', 'shard')), may hold values from 0 to 63, all different within a row; in each aligned block of 128 rows (0 to 127, 128 to 255, ...) at most 5 rows name the same one
- norm_attn: bfloat16 [2048], P(('expert', 'shard')), may hold values from 0.099609375 to 1.8984375
- w_query: bfloat16 [2048, 3072], P(('expert', 'shard')), may hold values from -0.1875 to 0.1875
- w_latent: bfloat16 [2048, 576], P(('expert', 'shard')), may hold values from -0.125 to 0.125
- norm_latent: bfloat16 [512], P(('expert', 'shard')), may hold values from 0.099609375 to 1.8984375
- w_expand: bfloat16 [512, 4096], P(('expert', 'shard')), may hold values from -0.25 to 0.25
- w_out: bfloat16 [2048, 2048], P(('expert', 'shard')), may hold values from -1 to 1
- norm_ffn: bfloat16 [2048], P(('expert', 'shard')), may hold values from 0.099609375 to 1.8984375
- w_router: bfloat16 [2048, 64], P(('expert', 'shard')), may hold values from -0.0625 to 0.0625
- w_shared_gate: bfloat16 [2048, 1408], P(('expert', 'shard')), may hold values from -0.125 to 0.125
- w_shared_up: bfloat16 [2048, 1408], P(('expert', 'shard')), may hold values from -0.125 to 0.125
- w_shared_down: bfloat16 [1408, 2048], P(('expert', 'shard')), may hold values from -0.15625 to 0.15625
- w_expert_gate: bfloat16 [64, 1408, 2048], P('expert', 'shard'), may hold values from -0.125 to 0.125
- w_expert_up: bfloat16 [64, 1408, 2048], P('expert', 'shard'), may hold values from -0.125 to 0.125
- w_expert_down: bfloat16 [64, 1408, 2048], P('expert', 'shard'), may hold values from -0.15625 to 0.15625
Outputs:
- layer_out: bfloat16 [16384, 2048], P(('expert', 'shard'))
- grad_input: float32 [16384, 2048], P(('expert', 'shard'))
- grad_norm_attn: float32 [2048], P(('expert', 'shard'))
- grad_query: float32 [2048, 3072], P(('expert', 'shard'))
- grad_latent: float32 [2048, 576], P(('expert', 'shard'))
- grad_norm_latent: float32 [512], P(('expert', 'shard'))
- grad_expand: float32 [512, 4096], P(('expert', 'shard'))
- grad_out: float32 [2048, 2048], P(('expert', 'shard'))
- grad_norm_ffn: float32 [2048], P(('expert', 'shard'))
- grad_router: float32 [2048, 64], P(('expert', 'shard'))
- grad_shared_gate: float32 [2048, 1408], P(('expert', 'shard'))
- grad_shared_up: float32 [2048, 1408], P(('expert', 'shard'))
- grad_shared_down: float32 [1408, 2048], P(('expert', 'shard'))
- grad_expert_gate: float32 [64, 1408, 2048], P('expert', 'shard')
- grad_expert_up: float32 [64, 1408, 2048], P('expert', 'shard')
- grad_expert_down: float32 [64, 1408, 2048], P('expert', 'shard')
Inputs may be any that keep to these rules, and one draw needn't show every extreme that they name: Each group's 3 lengths sum to 1024, and one of them is exactly 768. `dealing`: each row holds every place 0 to 1023 once. `routes`: a token names 2 different experts; among the rows of one device no expert is named more than 5 times, and 5 is reached.
All inputs are finite; a program needn't handle non-finite values.
Results may differ from a plain program's by a relative error of at most 0.03.
Values may be sent and summed in bfloat16 or wider, within the bound.
No kernel may reach another device: no remote copies, remote signals or barrier semaphores. Data moves between devices by JAX's collectives and lax.ppermute only.
A program may use at most 384 MiB of HBM per device.

v0:
```python
import jax
import jax.numpy as jnp
from jax import lax
from jax.sharding import PartitionSpec as P

H = 16
DN = 128
DR = 64
DV = 128
R = 512
EXP_DEV = 4
TOPK = 2


EPSILON = 1e-06
ROPE_BASE = 50000.0
ROUTE_SCALE = 2.446
MASKED = -1e30


def product(left, right):
    return jnp.dot(left, right, preferred_element_type=jnp.float32)


def product_tn(left, right):
    return lax.dot_general(
        left, right, (((0,), (0,)), ((), ())), preferred_element_type=jnp.float32
    )


def product_nt(left, right):
    return lax.dot_general(
        left, right, (((1,), (1,)), ((), ())), preferred_element_type=jnp.float32
    )


def rms_forward(value, gain):
    inverse = lax.rsqrt(jnp.mean(value * value, axis=-1, keepdims=True) + EPSILON)
    return (value * inverse * gain, inverse)


def rms_backward(value, inverse, gain, grad):
    weighted = grad * gain
    inner = jnp.mean(weighted * value, axis=-1, keepdims=True)
    value_grad = inverse * weighted - value * (inverse * inverse * inverse) * inner
    return (value_grad, jnp.sum(grad * value * inverse, axis=0))


def rope_tables(position, width):
    half_width = width // 2
    rates = ROPE_BASE ** (-2.0 * jnp.arange(half_width, dtype=jnp.float32) / width)
    angles = position.astype(jnp.float32)[:, None] * rates[None, :]
    return (jnp.cos(angles), jnp.sin(angles))


def rotate(value, cosine, sine_table):
    half_width = value.shape[-1] // 2
    front_half = value[..., :half_width]
    back_half = value[..., half_width:]
    return jnp.concatenate(
        [
            front_half * cosine - back_half * sine_table,
            back_half * cosine + front_half * sine_table,
        ],
        axis=-1,
    )


def silu_parts(value):
    logistic = jax.nn.sigmoid(value)
    return (value * logistic, logistic * (1.0 + value * (1.0 - logistic)))


def body(
    hidden_in,
    cotangent,
    lengths,
    dealing,
    routes,
    norm_attn,
    w_query,
    w_latent,
    norm_latent,
    w_expand,
    w_out,
    norm_ffn,
    w_router,
    w_shared_gate,
    w_shared_up,
    w_shared_down,
    w_expert_gate,
    w_expert_up,
    w_expert_down,
):
    local_rows = hidden_in.shape[0]
    model_width = hidden_in.shape[1]
    expert_axis = lax.axis_size("expert")
    expert_count = EXP_DEV * expert_axis
    capacity = max(2, 4 * local_rows * TOPK // (3 * expert_count))
    factor = (DN + DR) ** (-0.5)
    shards = (
        norm_attn,
        w_query,
        w_latent,
        norm_latent,
        w_expand,
        w_out,
        norm_ffn,
        w_router,
        w_shared_gate,
        w_shared_up,
        w_shared_down,
    )
    dense = (
        lax.all_gather(shards[0], ("expert", "shard"), axis=0, tiled=True),
        lax.all_gather(shards[1], ("expert", "shard"), axis=0, tiled=True),
        lax.all_gather(shards[2], ("expert", "shard"), axis=0, tiled=True),
        lax.all_gather(shards[3], ("expert", "shard"), axis=0, tiled=True),
        lax.all_gather(shards[4], ("expert", "shard"), axis=0, tiled=True),
        lax.all_gather(shards[5], ("expert", "shard"), axis=0, tiled=True),
        lax.all_gather(shards[6], ("expert", "shard"), axis=0, tiled=True),
        lax.all_gather(shards[7], ("expert", "shard"), axis=0, tiled=True),
        lax.all_gather(shards[8], ("expert", "shard"), axis=0, tiled=True),
        lax.all_gather(shards[9], ("expert", "shard"), axis=0, tiled=True),
        lax.all_gather(shards[10], ("expert", "shard"), axis=0, tiled=True),
    )
    (
        gain_attn,
        query_full,
        latent_full,
        gain_latent,
        expand_full,
        out_full,
        gain_ffn,
        router_full,
        shared_gate,
        shared_up,
        shared_down,
    ) = dense
    group_place = dealing[0]
    seq_lengths = lengths[0]
    seq_ends = jnp.cumsum(seq_lengths)
    seq_starts = seq_ends - seq_lengths
    seq_ids = jnp.arange(seq_lengths.shape[0], dtype=jnp.int32)
    key_segment = jnp.sum((group_place[:, None] >= seq_ends[None, :]).astype(jnp.int32), axis=1)
    my_first = lax.axis_index("shard") * local_rows
    query_place = lax.dynamic_slice_in_dim(group_place, my_first, local_rows)
    query_segment = lax.dynamic_slice_in_dim(key_segment, my_first, local_rows)
    position = query_place - jnp.sum(
        jnp.where(query_segment[:, None] == seq_ids[None, :], seq_starts[None, :], 0), axis=1
    )
    allowed = (query_segment[:, None] == key_segment[None, :]) & (
        group_place[None, :] <= query_place[:, None]
    )
    inputs32 = hidden_in.astype(jnp.float32)
    normed_f, inverse_in = rms_forward(inputs32, gain_attn.astype(jnp.float32))
    normed_in = normed_f.astype(jnp.bfloat16)
    query_proj = product(normed_in, query_full).reshape(local_rows, H, DN + DR)
    latent = product(normed_in, latent_full)
    compressed = latent[:, :R]
    latent_f, inverse_latent = rms_forward(compressed, gain_latent.astype(jnp.float32))
    latent_normed = latent_f.astype(jnp.bfloat16)
    cosine, sine_table = rope_tables(position, DR)
    key_rope = rotate(latent[:, R:], cosine, sine_table).astype(jnp.bfloat16)
    queries = jnp.concatenate(
        [
            query_proj[..., :DN],
            rotate(query_proj[..., DN:], cosine[:, None, :], sine_table[:, None, :]),
        ],
        axis=-1,
    ).astype(jnp.bfloat16)
    expanded = product(latent_normed, expand_full).astype(jnp.bfloat16)
    group_expanded, group_rope = (
        lax.all_gather(expanded, "shard", axis=0, tiled=True),
        lax.all_gather(key_rope, "shard", axis=0, tiled=True),
    )
    group_kv = group_expanded.reshape(group_expanded.shape[0], H, DN + DV)
    key_nope = group_kv[..., :DN]
    values = group_kv[..., DN:]

    def attention_scores():
        raw = jnp.einsum(
            "qhc,khc->hqk", queries[..., :DN], key_nope, preferred_element_type=jnp.float32
        )
        raw = raw + jnp.einsum(
            "qhc,kc->hqk", queries[..., DN:], group_rope, preferred_element_type=jnp.float32
        )
        return jnp.where(allowed[None], raw * factor, MASKED)

    masked = attention_scores()
    row_peak = jnp.max(masked, axis=-1, keepdims=True)
    weights = jnp.exp(masked - row_peak)
    totals = jnp.sum(weights, axis=-1, keepdims=True)
    attention_probs = weights / totals
    log_total = row_peak + jnp.log(totals)
    mixed_heads = jnp.einsum(
        "hqk,khv->qhv",
        attention_probs.astype(jnp.bfloat16),
        values,
        preferred_element_type=jnp.float32,
    )
    attended = mixed_heads.reshape(local_rows, H * DV).astype(jnp.bfloat16)
    middle = inputs32 + product(attended, out_full)
    mid_f, inverse_mid = rms_forward(middle, gain_ffn.astype(jnp.float32))
    normed_mid = mid_f.astype(jnp.bfloat16)
    logits = product(normed_mid, router_full)
    route_hot = (
        routes[:, :, None] == jnp.arange(expert_count, dtype=jnp.int32)[None, None, :]
    ).astype(jnp.float32)
    chosen = jnp.sum(route_hot * logits[:, None, :], axis=-1)
    scores_sig = jax.nn.sigmoid(chosen)
    sig_total = jnp.sum(scores_sig, axis=1, keepdims=True)
    gate_values = ROUTE_SCALE * scores_sig / sig_total
    shared_a = product(normed_mid, shared_gate)
    shared_b = product(normed_mid, shared_up)
    silu_shared, slope_shared = silu_parts(shared_a)
    shared_hidden = (silu_shared * shared_b).astype(jnp.bfloat16)
    shared_out = product(shared_hidden, shared_down)
    flat_expert = routes.reshape(-1)
    flat_hot = (flat_expert[:, None] == jnp.arange(expert_count, dtype=jnp.int32)[None, :]).astype(
        jnp.int32
    )
    slot_rank = jnp.sum(flat_hot * jnp.cumsum(flat_hot, axis=0), axis=1) - 1
    flat_owner = flat_expert // EXP_DEV
    flat_local = flat_expert % EXP_DEV
    send_column = flat_owner * capacity + slot_rank
    return_index = send_column * EXP_DEV + flat_local
    own_slots = expert_axis * capacity

    def pack(rows_flat):
        buffer = jnp.zeros((EXP_DEV, own_slots, model_width), jnp.bfloat16)
        return buffer.at[flat_local, send_column].set(rows_flat)

    outbound = pack(jnp.repeat(normed_mid, TOPK, axis=0))
    inbound = lax.all_to_all(outbound, "expert", split_axis=1, concat_axis=1, tiled=True)
    expert_rows = lax.all_gather(inbound, "shard", axis=1, tiled=True)
    gate_pre = jnp.einsum(
        "jsd,jfd->jsf", expert_rows, w_expert_gate, preferred_element_type=jnp.float32
    )
    up_pre = jnp.einsum(
        "jsd,jfd->jsf", expert_rows, w_expert_up, preferred_element_type=jnp.float32
    )
    silu_gate, slope_gate = silu_parts(gate_pre)
    expert_hidden = (silu_gate * up_pre).astype(jnp.bfloat16)
    expert_sums = lax.psum_scatter(
        jnp.einsum(
            "jsf,jfd->sjd", expert_hidden, w_expert_down, preferred_element_type=jnp.float32
        ).astype(jnp.bfloat16),
        "shard",
        scatter_dimension=0,
        tiled=True,
    )
    returned = lax.all_to_all(expert_sums, "expert", split_axis=0, concat_axis=0, tiled=True)
    route_out = (
        jnp.take(returned.reshape(-1, model_width), return_index, axis=0)
        .reshape(local_rows, TOPK, model_width)
        .astype(jnp.float32)
    )
    mixture = jnp.sum(gate_values[:, :, None] * route_out, axis=1)
    layer_out = (middle + shared_out + mixture).astype(jnp.bfloat16)
    (
        attn_gain_b,
        query_w,
        latent_w,
        latent_gain_b,
        expand_w,
        out_w,
        ffn_gain_b,
        router_w,
        gate_w,
        up_w,
        down_w,
    ) = dense
    grad_top = cotangent.astype(jnp.float32)
    route_grad = (gate_values[:, :, None] * grad_top[:, None, :]).astype(jnp.bfloat16)
    outbound_grad = pack(route_grad.reshape(local_rows * TOPK, model_width))
    inbound_grad = lax.all_to_all(outbound_grad, "expert", split_axis=1, concat_axis=1, tiled=True)
    expert_grad = lax.all_gather(inbound_grad, "shard", axis=1, tiled=True)
    hidden_grad = jnp.einsum(
        "jsd,jfd->jsf", expert_grad, w_expert_down, preferred_element_type=jnp.float32
    )
    grad_gate_pre = (hidden_grad * up_pre * slope_gate).astype(jnp.bfloat16)
    grad_up_pre = (hidden_grad * silu_gate).astype(jnp.bfloat16)
    grad_expert_down = jnp.einsum(
        "jsf,jsd->jfd", expert_hidden, expert_grad, preferred_element_type=jnp.float32
    )
    grad_expert_gate = jnp.einsum(
        "jsf,jsd->jfd", grad_gate_pre, expert_rows, preferred_element_type=jnp.float32
    )
    grad_expert_up = jnp.einsum(
        "jsf,jsd->jfd", grad_up_pre, expert_rows, preferred_element_type=jnp.float32
    )
    gate_term = jnp.einsum(
        "jsf,jfd->sjd", grad_gate_pre, w_expert_gate, preferred_element_type=jnp.float32
    )
    row_sums = lax.psum_scatter(
        (
            gate_term
            + jnp.einsum(
                "jsf,jfd->sjd", grad_up_pre, w_expert_up, preferred_element_type=jnp.float32
            )
        ).astype(jnp.bfloat16),
        "shard",
        scatter_dimension=0,
        tiled=True,
    )
    returned_grad = lax.all_to_all(row_sums, "expert", split_axis=0, concat_axis=0, tiled=True)
    route_back = jnp.take(returned_grad.reshape(-1, model_width), return_index, axis=0).astype(
        jnp.float32
    )
    grad_routes = jnp.sum(route_back.reshape(local_rows, TOPK, model_width), axis=1)
    gate_grad = jnp.sum(grad_top[:, None, :] * route_out, axis=-1)
    weighted_sum = jnp.sum(gate_grad * gate_values, axis=1, keepdims=True)
    sig_grad = ROUTE_SCALE / sig_total * (gate_grad - weighted_sum / ROUTE_SCALE)
    chosen_grad = sig_grad * scores_sig * (1.0 - scores_sig)
    logit_grad = jnp.sum(route_hot * chosen_grad[:, :, None], axis=1).astype(jnp.bfloat16)
    grad_router = product_tn(normed_mid, logit_grad)
    shared_grad = grad_top.astype(jnp.bfloat16)
    shared_hidden_grad = product_nt(shared_grad, down_w)
    grad_shared_a = (shared_hidden_grad * shared_b * slope_shared).astype(jnp.bfloat16)
    grad_shared_b = (shared_hidden_grad * silu_shared).astype(jnp.bfloat16)
    grad_shared_down = product_tn(shared_hidden, shared_grad)
    grad_shared_gate = product_tn(normed_mid, grad_shared_a)
    grad_shared_up = product_tn(normed_mid, grad_shared_b)
    normed_grad = (
        product_nt(logit_grad, router_w)
        + product_nt(grad_shared_a, gate_w)
        + product_nt(grad_shared_b, up_w)
        + grad_routes
    )
    middle_norm_grad, grad_gain_ffn = rms_backward(
        middle, inverse_mid, ffn_gain_b.astype(jnp.float32), normed_grad
    )
    middle_grad = grad_top + middle_norm_grad
    attn_grad = middle_grad.astype(jnp.bfloat16)
    grad_out_proj = product_tn(attended, attn_grad)
    attended_grad = product_nt(attn_grad, out_w).astype(jnp.bfloat16).reshape(local_rows, H, DV)
    masked = attention_scores()
    attention_probs = jnp.exp(masked - log_total)
    probs_grad = jnp.einsum(
        "qhv,khv->hqk", attended_grad, values, preferred_element_type=jnp.float32
    )
    value_grad = jnp.einsum(
        "hqk,qhv->khv",
        attention_probs.astype(jnp.bfloat16),
        attended_grad,
        preferred_element_type=jnp.float32,
    )
    inner = jnp.sum(attention_probs * probs_grad, axis=-1, keepdims=True)
    score_grad = (attention_probs * (probs_grad - inner)).astype(jnp.bfloat16)
    query_grad_nope = (
        jnp.einsum("hqk,khc->qhc", score_grad, key_nope, preferred_element_type=jnp.float32)
        * factor
    )
    query_grad_rope = (
        jnp.einsum("hqk,kc->qhc", score_grad, group_rope, preferred_element_type=jnp.float32)
        * factor
    )
    key_grad_nope = (
        jnp.einsum(
            "hqk,qhc->khc", score_grad, queries[..., :DN], preferred_element_type=jnp.float32
        )
        * factor
    )
    key_grad_rope = (
        jnp.einsum("hqk,qhc->kc", score_grad, queries[..., DN:], preferred_element_type=jnp.float32)
        * factor
    )
    group_grad = jnp.concatenate([key_grad_nope, value_grad], axis=-1).reshape(
        key_grad_nope.shape[0], H * (DN + DV)
    )
    own_kv_grad, own_rope_grad = (
        lax.psum_scatter(
            group_grad.astype(jnp.bfloat16), "shard", scatter_dimension=0, tiled=True
        ).astype(jnp.float32),
        lax.psum_scatter(
            key_grad_rope.astype(jnp.bfloat16), "shard", scatter_dimension=0, tiled=True
        ).astype(jnp.float32),
    )
    expand_grad = own_kv_grad.astype(jnp.bfloat16)
    grad_expand = product_tn(latent_normed, expand_grad)
    latent_normed_grad = product_nt(expand_grad, expand_w)
    compressed_grad, grad_gain_latent = rms_backward(
        compressed, inverse_latent, latent_gain_b.astype(jnp.float32), latent_normed_grad
    )
    rope_grad = rotate(own_rope_grad, cosine, -sine_table)
    latent_grad = jnp.concatenate([compressed_grad, rope_grad], axis=-1).astype(jnp.bfloat16)
    query_grad = jnp.concatenate(
        [query_grad_nope, rotate(query_grad_rope, cosine[:, None, :], -sine_table[:, None, :])],
        axis=-1,
    )
    query_grad = query_grad.reshape(local_rows, H * (DN + DR)).astype(jnp.bfloat16)
    grad_query = product_tn(normed_in, query_grad)
    grad_latent = product_tn(normed_in, latent_grad)
    normed_in_grad = product_nt(query_grad, query_w) + product_nt(latent_grad, latent_w)
    input_norm_grad, grad_gain_attn = rms_backward(
        inputs32, inverse_in, attn_gain_b.astype(jnp.float32), normed_in_grad
    )
    grad_input = middle_grad + input_norm_grad
    summed = (
        lax.psum_scatter(grad_gain_attn, ("expert", "shard"), scatter_dimension=0, tiled=True),
        lax.psum_scatter(grad_query, ("expert", "shard"), scatter_dimension=0, tiled=True),
        lax.psum_scatter(grad_latent, ("expert", "shard"), scatter_dimension=0, tiled=True),
        lax.psum_scatter(grad_gain_latent, ("expert", "shard"), scatter_dimension=0, tiled=True),
        lax.psum_scatter(grad_expand, ("expert", "shard"), scatter_dimension=0, tiled=True),
        lax.psum_scatter(grad_out_proj, ("expert", "shard"), scatter_dimension=0, tiled=True),
        lax.psum_scatter(grad_gain_ffn, ("expert", "shard"), scatter_dimension=0, tiled=True),
        lax.psum_scatter(grad_router, ("expert", "shard"), scatter_dimension=0, tiled=True),
        lax.psum_scatter(grad_shared_gate, ("expert", "shard"), scatter_dimension=0, tiled=True),
        lax.psum_scatter(grad_shared_up, ("expert", "shard"), scatter_dimension=0, tiled=True),
        lax.psum_scatter(grad_shared_down, ("expert", "shard"), scatter_dimension=0, tiled=True),
    )
    return (
        layer_out,
        grad_input,
        summed[0],
        summed[1],
        summed[2],
        summed[3],
        summed[4],
        summed[5],
        summed[6],
        summed[7],
        summed[8],
        summed[9],
        summed[10],
        grad_expert_gate,
        grad_expert_up,
        grad_expert_down,
    )


def solution(mesh):
    placed = (
        P(("expert", "shard"), None),
        P(("expert", "shard"), None),
        P("expert", None),
        P("expert", None),
        P(("expert", "shard"), None),
        P(("expert", "shard")),
        P(("expert", "shard"), None),
        P(("expert", "shard"), None),
        P(("expert", "shard")),
        P(("expert", "shard"), None),
        P(("expert", "shard"), None),
        P(("expert", "shard")),
        P(("expert", "shard"), None),
        P(("expert", "shard"), None),
        P(("expert", "shard"), None),
        P(("expert", "shard"), None),
        P("expert", "shard", None),
        P("expert", "shard", None),
        P("expert", "shard", None),
    )
    return jax.shard_map(
        body,
        mesh=mesh,
        in_specs=placed,
        out_specs=(
            P(("expert", "shard"), None),
            P(("expert", "shard"), None),
            P(("expert", "shard")),
            P(("expert", "shard"), None),
            P(("expert", "shard"), None),
            P(("expert", "shard")),
            P(("expert", "shard"), None),
            P(("expert", "shard"), None),
            P(("expert", "shard")),
            P(("expert", "shard"), None),
            P(("expert", "shard"), None),
            P(("expert", "shard"), None),
            P(("expert", "shard"), None),
            P("expert", "shard", None),
            P("expert", "shard", None),
            P("expert", "shard", None),
        ),
        check_vma=False,
    )
```

profile of v0, /device:TPU:8, one launch (start us, length us, event | category | flops | bytes accessed | tf_op | source)
XLA Modules:
  0.0 4916.3 jit_solution(5869582556415625148)
XLA Ops:
  11.3 67.6 %all-reduce.10 = (bf16[2048]{0:T(1024)(128)(2,1)S(1)}, bf16[512]{0:T(512)(128)(2,1)S(1)}, bf16[2048]{0:T(1024)(128)(2,1)S(1)}) all-reduce(bf16[2048]{0:T(1024)(128)(2,1)S(1)} %dynamic-update-slice, bf16[512]{0:T(512)(128)(2,1)S(1)} %dynamic-update-slice.1, ...), channel_id=1, replica_groups=mesh['expert'=16,'shard'=8] {'expert','shard'}, use_global_device_ids=true, to_apply=%add | all-reduce | flops 4608 | bytes 18432
  84.4 60.8 %all-gather.29.cloned.1.call-done = bf16[128,4,4096]{2,1,0:T(4,128)(2,1)} async-done(((bf16[1,4,4096]{2,1,0:T(4,128)(2,1)}), bf16[128,4,4096]{2,1,0:T(4,128)(2,1)}) %all-gather.29.cloned.1.call-update) | async-done | bytes 4194320 | tf_op jit(solution)/shard_map/all_gather | solution.py:119
  161.7 11.4 all_gather.51
  173.1 30.9 all-gather.15.cloned.1.call-done
  204.0 9.8 copy.181
  227.0 54.3 %all-gather.17.cloned.1.call-done = bf16[2048,3072]{1,0:T(8,128)(2,1)} async-done(((bf16[16,3072]{1,0:T(8,128)(2,1)}), bf16[2048,3072]{1,0:T(8,128)(2,1)}) %all-gather.17.cloned.1.call-update) | async-done | bytes 12582928 | tf_op jit(solution)/shard_map/all_gather | solution.py:116
  304.4 48.1 all-gather.19.cloned.1.call-done
  363.6 46.4 scatter_fusion
  412.4 24.4 all_to_all.20
  438.7 55.9 %all-gather.25.cloned.1.call-done = bf16[4,640,2048]{2,1,0:T(8,128)(2,1)} async-done(((bf16[4,80,2048]{2,1,0:T(8,128)(2,1)}), bf16[4,640,2048]{2,1,0:T(8,128)(2,1)}) %all-gather.25.cloned.1.call-update) | async-done | bytes 10485776 | tf_op jit(solution)/shard_map/all_gather | solution.py:236
  494.6 9.6 fusion.96
  504.2 9.5 multiply_convert_fusion.5
  520.6 61.1 %reduce-scatter.17.cloned.1.call-done = bf16[80,4,2048]{2,0,1:T(8,128)(2,1)} async-done(((bf16[640,4,2048]{2,0,1:T(8,128)(2,1)}), bf16[80,4,2048]{2,0,1:T(8,128)(2,1)}) %reduce-scatter.17.cloned.1.call-update) | async-done | bytes 1310736 | tf_op jit(solution)/shard_map/reduce_scatter | solution.py:245
  600.0 37.3 all_gather.57
  653.5 46.2 scatter_fusion.1
  702.0 25.3 all_to_all.21
  731.4 53.3 %all-gather.27.cloned.1.call-done = bf16[4,640,2048]{2,1,0:T(8,128)(2,1)} async-done(((bf16[4,80,2048]{2,1,0:T(8,128)(2,1)}), bf16[4,640,2048]{2,1,0:T(8,128)(2,1)}) %all-gather.27.cloned.1.call-update) | async-done | bytes 10485776 | tf_op jit(solution)/shard_map/all_gather | solution.py:278
  784.7 9.9 multiply_convert_fusion.3
  794.6 12.2 fusion.97
  806.8 12.1 fusion.1
  818.9 38.6 all-gather.31.cloned.1.call-done
  866.5 59.4 %all-gather.21.cloned.1.call-done = bf16[2048,1408]{1,0:T(8,128)(2,1)} async-done(((bf16[16,1408]{1,0:T(8,128)(2,1)}), bf16[2048,1408]{1,0:T(8,128)(2,1)}) %all-gather.21.cloned.1.call-update) | async-done | bytes 5767184 | tf_op jit(solution)/shard_map/all_gather | solution.py:123
  929.5 64.7 %all-gather.23.cloned.1.call-done = bf16[2048,1408]{1,0:T(8,128)(2,1)} async-done(((bf16[16,1408]{1,0:T(8,128)(2,1)}), bf16[2048,1408]{1,0:T(8,128)(2,1)}) %all-gather.23.cloned.1.call-update) | async-done | bytes 5767184 | tf_op jit(solution)/shard_map/all_gather | solution.py:124
  1001.5 53.7 %reduce-scatter.19.cloned.1.call-done = bf16[80,4,2048]{2,0,1:T(8,128)(2,1)} async-done(((bf16[640,4,2048]{2,0,1:T(8,128)(2,1)}), bf16[80,4,2048]{2,0,1:T(8,128)(2,1)}) %reduce-scatter.19.cloned.1.call-update) | async-done | bytes 1310736 | tf_op jit(solution)/shard_map/reduce_scatter | solution.py:296
  1071.9 16.0 all-to-all-done.3
  1146.5 11.5 copy.173
  1162.9 43.8 reduce-scatter.33.cloned.1.call-done
  1227.9 10.6 reduce-scatter.35.cloned.1.call-done
  1267.0 10.8 fusion.84
  1284.9 378.7 %fusion = f32[16,2048]{1,0:T(8,128)S(1)} fusion(f32[1408,2048]{1,0:T(8,128)} %fusion.101), kind=kCustom, calls=%all-reduce-scatter | all-reduce-scatter fusion | flops 4194305 | bytes 11665408
  1670.2 13.1 collective-permute-done.39
  1722.7 11.2 collective-permute-start.21
  1780.4 10.0 collective-permute-start.7
  1790.5 10.2 collective-permute-start.6
  1800.7 10.2 collective-permute-start.5
  1810.9 10.8 collective-permute-start.4
  1821.8 10.2 collective-permute-start.3
  1832.0 10.2 collective-permute-start.2
  1842.2 9.6 collective-permute-start.1
  1851.8 10.2 collective-permute-start
  1864.8 67.1 %concatenate.35 = f32[651,2048]{1,0:T(8,128)} concatenate(f32[11,2048]{1,0:T(8,128)S(1)} %collective-permute-done.39, f32[16,2048]{1,0:T(8,128)S(1)} %collective-permute-done.38, f32[16,2048]{1,0:T(8,128)S(1)} %collective-permute-done.37, f32[16,2048]{1,0:T(8,128)S(1)} %collective-permute-done.36, f32[16,2048]{1,0:T(8,128)S(1)} %collective-permute-done.35, ...), dimensions={0} | concatenate | bytes 10665984
  1981.7 69.1 %all-reduce.9 = (f32[2048]{0:T(1024)S(1)}, f32[512]{0:T(512)S(1)}, f32[2048]{0:T(1024)S(1)}) all-reduce(f32[2048]{0:T(1024)} %get-tuple-element.19, f32[512]{0:T(512)} %get-tuple-element.21, f32[2048]{0:T(1024)} %get-tuple-element.17), channel_id=6, replica_groups=mesh['expert'=16,'shard'=8] {'expert','shard'}, use_global_device_ids=true, to_apply=%region_29.31.clone | all-reduce | flops 4608 | bytes 36864
  2057.8 11.4 reduce-scatter.29.cloned.1.call-done
  2069.1 652.1 %reduce-scatter.31.cloned.1.call-done = f32[16,1408]{1,0:T(8,128)} async-done(((f32[2048,1408]{1,0:T(8,128)}), f32[16,1408]{1,0:T(8,128)}) %reduce-scatter.31.cloned.1.call-update) | async-done | bytes 90128 | tf_op jit(solution)/shard_map/reduce_scatter | solution.py:410
  2721.2 633.8 %reduce-scatter.27.cloned.1.call-done = f32[16,64]{1,0:T(8,128)} async-done(((f32[2048,64]{1,0:T(8,128)}), f32[16,64]{1,0:T(8,128)}) %reduce-scatter.27.cloned.1.call-update) | async-done | bytes 4112 | tf_op jit(solution)/shard_map/reduce_scatter | solution.py:408
  3354.9 640.5 %reduce-scatter.23.cloned.1.call-done = f32[16,576]{1,0:T(8,128)} async-done(((f32[2048,576]{1,0:T(8,128)}), f32[16,576]{1,0:T(8,128)}) %reduce-scatter.23.cloned.1.call-update) | async-done | bytes 36880 | tf_op jit(solution)/shard_map/reduce_scatter | solution.py:403
  3995.4 661.5 %reduce-scatter.25.cloned.1.call-done = f32[16,2048]{1,0:T(8,128)} async-done(((f32[2048,2048]{1,0:T(8,128)}), f32[16,2048]{1,0:T(8,128)}) %reduce-scatter.25.cloned.1.call-update) | async-done | bytes 131088 | tf_op jit(solution)/shard_map/reduce_scatter | solution.py:406
  4656.9 252.4 %reduce-scatter.21.cloned.1.call-done = f32[16,3072]{1,0:T(8,128)} async-done(((f32[2048,3072]{1,0:T(8,128)}), f32[16,3072]{1,0:T(8,128)}) %reduce-scatter.21.cloned.1.call-update) | async-done | bytes 196624 | tf_op jit(solution)/shard_map/reduce_scatter | solution.py:402
  (473 shorter events, 432.3 us)
Async XLA Ops:
  7.2 73.5 %all-gather.13.cloned.1.call-start = ((), (), s32[]{:S(2)}) async-start(), calls=%async_computation.14 | async-start | bytes 2641920 | tf_op jit(solution)/shard_map/all_gather | solution.py:117
  7.9 137.3 %all-gather.29.cloned.1.call-start = ((), (), s32[]{:S(2)}) async-start(), calls=%async_computation.30 | async-start | bytes 4227072 | tf_op jit(solution)/shard_map/all_gather | solution.py:119
  8.7 195.3 %all-gather.15.cloned.1.call-start = ((), (), s32[]{:S(2)}) async-start(), calls=%async_computation.15 | async-start | bytes 9437184 | tf_op jit(solution)/shard_map/all_gather | solution.py:174
  156.2 125.1 %all-gather.17.cloned.1.call-start = ((), (), s32[]{:S(2)}) async-start(), calls=%async_computation.16 | async-start | bytes 12681216 | tf_op jit(solution)/shard_map/all_gather | solution.py:116
  156.8 195.8 %all-gather.19.cloned.1.call-start = ((), (), s32[]{:S(2)}) async-start(), calls=%async_computation.17 | async-start | bytes 8454144 | tf_op jit(solution)/shard_map/all_gather | solution.py:120
  157.3 337.2 %all-gather.25.cloned.1.call-start = ((), (), s32[]{:S(2)}) async-start(), calls=%async_computation.20 | async-start | bytes 11796480 | tf_op jit(solution)/shard_map/all_gather | solution.py:236
  438.6 143.0 %reduce-scatter.17.cloned.1.call-start = ((), (), s32[]{:S(2)}) async-start(), calls=%async_computation.21 | async-start | bytes 11796480 | tf_op jit(solution)/shard_map/reduce_scatter | solution.py:245
  585.1 53.4 %all-to-all-start.1 = ((bf16[80,4,2048]{2,1,0:T(4,128)(2,1)}), bf16[80,4,2048]{2,1,0:T(4,128)(2,1)}, u32[]{:S(2)}, u32[]{:S(2)}) async-start(bf16[80,4,2048]{2,1,0:T(4,128)(2,1)} %copy.154), calls=%async_computation.2 | async-start | bytes 2621440 | tf_op jit(solution)/shard_map/all_to_all | solution.py:253
  592.4 192.3 %all-gather.27.cloned.1.call-start = ((), (), s32[]{:S(2)}) async-start(), calls=%async_computation.22 | async-start | bytes 11796480 | tf_op jit(solution)/shard_map/all_gather | solution.py:278
  729.1 128.5 %all-gather.31.cloned.1.call-start = ((), (), s32[]{:S(2)}) async-start(), calls=%async_computation.31 | async-start | bytes 8454144 | tf_op jit(solution)/shard_map/all_gather | solution.py:125
  729.8 196.0 %all-gather.21.cloned.1.call-start = ((), (), s32[]{:S(2)}) async-start(), calls=%async_computation.18 | async-start | bytes 5812224 | tf_op jit(solution)/shard_map/all_gather | solution.py:123
  730.4 263.8 %all-gather.23.cloned.1.call-start = ((), (), s32[]{:S(2)}) async-start(), calls=%async_computation.19 | async-start | bytes 5812224 | tf_op jit(solution)/shard_map/all_gather | solution.py:124
  731.1 324.1 %reduce-scatter.19.cloned.1.call-start = ((), (), s32[]{:S(2)}) async-start(), calls=%async_computation.23 | async-start | bytes 11796480 | tf_op jit(solution)/shard_map/reduce_scatter | solution.py:296
  1058.6 29.2 all-to-all-start.3
  1065.8 140.9 %reduce-scatter.33.cloned.1.call-start = ((), (), s32[]{:S(2)}) async-start(), calls=%async_computation.32 | async-start | bytes 9437184
  1158.0 80.4 %reduce-scatter.35.cloned.1.call-start = ((), (), s32[]{:S(2)}) async-start(), calls=%async_computation.33 | async-start | bytes 294912
  1162.9 893.3 %all-reduce.13.cloned.1.call-start = ((), (), s32[]{:S(2)}) async-start(), calls=%async_computation.34 | async-start | bytes 16777216
  1212.6 856.5 %reduce-scatter.29.cloned.1.call-start = ((), (), s32[]{:S(2)}) async-start(), calls=%async_computation.28 | async-start | bytes 11624448 | tf_op jit(solution)/shard_map/reduce_scatter | solution.py:409
  1219.5 1501.6 %reduce-scatter.31.cloned.1.call-start = ((), (), s32[]{:S(2)}) async-start(), calls=%async_computation.29 | async-start | bytes 11624448 | tf_op jit(solution)/shard_map/reduce_scatter | solution.py:410
  1226.5 2128.5 %reduce-scatter.27.cloned.1.call-start = ((), (), s32[]{:S(2)}) async-start(), calls=%async_computation.27 | async-start | bytes 1056768 | tf_op jit(solution)/shard_map/reduce_scatter | solution.py:408
  1227.9 2767.5 %reduce-scatter.23.cloned.1.call-start = ((), (), s32[]{:S(2)}) async-start(), calls=%async_computation.25 | async-start | bytes 5283840 | tf_op jit(solution)/shard_map/reduce_scatter | solution.py:403
  1247.4 3409.6 %reduce-scatter.25.cloned.1.call-start = ((), (), s32[]{:S(2)}) async-start(), calls=%async_computation.26 | async-start | bytes 16908288 | tf_op jit(solution)/shard_map/reduce_scatter | solution.py:406
  1257.1 3652.2 %reduce-scatter.21.cloned.1.call-start = ((), (), s32[]{:S(2)}) async-start(), calls=%async_computation.24 | async-start | bytes 25362432 | tf_op jit(solution)/shard_map/reduce_scatter | solution.py:402
  1663.6 21.0 collective-permute-start.38
  1664.9 21.0 collective-permute-start.37
  1666.2 21.0 collective-permute-start.36
  1667.5 21.0 collective-permute-start.35
  1687.2 21.9 collective-permute-start.31
  1688.5 24.7 collective-permute-start.30
  1691.3 23.6 collective-permute-start.29
  1695.1 21.7 collective-permute-start.28
  1714.9 24.3 collective-permute-start.24
  1716.9 23.7 collective-permute-start.23
  1719.1 22.8 collective-permute-start.22
  1722.7 24.6 collective-permute-start.21
  1741.9 21.2 collective-permute-start.17
  1748.7 23.5 collective-permute-start.15
  1750.0 24.4 collective-permute-start.14
  1767.1 23.4 collective-permute-start.11
  1772.2 28.5 collective-permute-start.10
  1774.5 36.4 collective-permute-start.9
  1779.1 42.6 collective-permute-start.8
  1780.4 51.5 %collective-permute-start.7 = (f32[16,2048]{1,0:T(8,128)S(1)}, f32[16,2048]{1,0:T(8,128)S(1)}, u32[]{:S(2)}, u32[]{:S(2)}) collective-permute-start(f32[16,2048]{1,0:T(8,128)S(1)} %fusion), channel_id=1, source_target_pairs={{0,8},{1,9},{2,10},{3,11},{4,12},{5,13},{6,14},{7,15},{8,16},{9,17... | collective-permute-start | bytes 393224
  1790.5 51.7 %collective-permute-start.6 = (f32[16,2048]{1,0:T(8,128)S(1)}, f32[16,2048]{1,0:T(8,128)S(1)}, u32[]{:S(2)}, u32[]{:S(2)}) collective-permute-start(f32[16,2048]{1,0:T(8,128)S(1)} %fusion), channel_id=1, source_target_pairs={{0,7},{1,8},{2,9},{3,10},{4,11},{5,12},{6,13},{7,14},{8,15},{9,16}... | collective-permute-start | bytes 393224
  1800.7 51.0 %collective-permute-start.5 = (f32[16,2048]{1,0:T(8,128)S(1)}, f32[16,2048]{1,0:T(8,128)S(1)}, u32[]{:S(2)}, u32[]{:S(2)}) collective-permute-start(f32[16,2048]{1,0:T(8,128)S(1)} %fusion), channel_id=1, source_target_pairs={{0,6},{1,7},{2,8},{3,9},{4,10},{5,11},{6,12},{7,13},{8,14},{9,15},... | collective-permute-start | bytes 393224
  1810.9 51.3 %collective-permute-start.4 = (f32[16,2048]{1,0:T(8,128)S(1)}, f32[16,2048]{1,0:T(8,128)}, u32[]{:S(2)}, u32[]{:S(2)}) collective-permute-start(f32[16,2048]{1,0:T(8,128)S(1)} %fusion), channel_id=1, source_target_pairs={{0,5},{1,6},{2,7},{3,8},{4,9},{5,10},{6,11},{7,12},{8,13},{9,14},{... | collective-permute-start | bytes 393224
  1821.8 40.5 collective-permute-start.3
  1832.0 30.3 collective-permute-start.2
  (124 other events, 8833.0 us)
Sparse Core Ops, SparseCore 0:
  11.2 66.5 all-gather.12
  81.0 64.2 all-gather.28
  156.3 47.6 all-gather.14
  207.0 74.2 all-gather.16
  284.1 68.3 all-gather.18
  438.8 55.7 all-gather.24
  520.7 60.9 reduce-scatter.16
  729.2 55.4 all-gather.26
  787.7 69.8 all-gather.30
  860.4 65.4 all-gather.20
  928.8 65.3 all-gather.22
  996.5 58.6 reduce-scatter.18
  1158.1 48.5 reduce-scatter.32
  1208.9 29.5 reduce-scatter.34
  1244.2 164.4 all-reduce.12
  1411.5 657.6 reduce-scatter.28
  2071.9 649.1 reduce-scatter.30
  2723.9 630.9 reduce-scatter.26
  3358.0 637.3 reduce-scatter.22
  3998.2 658.6 reduce-scatter.24
  4662.8 246.4 reduce-scatter.20
where the time goes:
time: 4930 us; the launch traced here: 4920 us
  waiting for transfers between devices  3530 us (72%)
  blocking collectives  614 us (12%)
  local copies, waits for them, and re-layouts  282 us (6%)
  matrix products  241 us (5%)
  starting transfers between devices  196 us (4%)
    reduce_scatter x1, waiting for transfers between devices, body(): lax.psum_scatter(grad_out_proj, ('expert', 'shard'), scatter_dimension=0,...  662 us
    reduce_scatter x1, waiting for transfers between devices, body(): lax.psum_scatter(grad_shared_up, ('expert', 'shard'), scatter_dimension=0...  652 us
    reduce_scatter x1, waiting for transfers between devices, body(): lax.psum_scatter(grad_latent, ('expert', 'shard'), scatter_dimension=0, t...  640 us
    reduce_scatter x1, waiting for transfers between devices, body(): lax.psum_scatter(grad_router, ('expert', 'shard'), scatter_dimension=0, t...  634 us
    unnamed x3, blocking collectives  515 us
    reduce_scatter x1, waiting for transfers between devices, body(): lax.psum_scatter(grad_query, ('expert', 'shard'), scatter_dimension=0, ti...  252 us
    unnamed x43, starting transfers between devices  180 us
    unnamed x239, local copies, waits for them, and re-layouts  134 us
  transfers between devices with their start and end apart: 63, of which 24 were waited for; matrix products, arithmetic and copies ran while one was open for 14% of the time, Pallas kernels for 0%

commit v1 on v0

v1 whole, which is shorter than its diff:
```python
import jax
import jax.numpy as jnp
from jax import lax
from jax.experimental import pallas as pl
from jax.experimental.pallas import tpu as pltpu
from jax.sharding import PartitionSpec as P

H = 16
DN = 128
DR = 64
DV = 128
R = 512
EXP_DEV = 4
TOPK = 2
CAP = 5
N_EXPERT = 16
N_SHARD = 8
SLOT = 24
HEADS = H // N_SHARD
QW = HEADS * (DN + DR)
KVW = HEADS * (DN + DV)
LW = R + DR

EPSILON = 1e-06
ROPE_BASE = 50000.0
ROUTE_SCALE = 2.446
MASKED = -1e30
BF = jnp.bfloat16
F32 = jnp.float32


def product(left, right):
    return jnp.dot(left, right, preferred_element_type=F32)


def product_tn(left, right):
    return lax.dot_general(left, right, (((0,), (0,)), ((), ())), preferred_element_type=F32)


def product_nt(left, right):
    return lax.dot_general(left, right, (((1,), (1,)), ((), ())), preferred_element_type=F32)


def rms_forward(value, gain):
    inverse = lax.rsqrt(jnp.mean(value * value, axis=-1, keepdims=True) + EPSILON)
    return (value * inverse * gain, inverse)


def rms_backward(value, inverse, gain, grad):
    weighted = grad * gain
    inner = jnp.mean(weighted * value, axis=-1, keepdims=True)
    value_grad = inverse * weighted - value * (inverse * inverse * inverse) * inner
    return (value_grad, jnp.sum(grad * value * inverse, axis=0))


def rope_tables(position, width):
    half_width = width // 2
    rates = ROPE_BASE ** (-2.0 * jnp.arange(half_width, dtype=F32) / width)
    angles = position.astype(F32)[:, None] * rates[None, :]
    return (jnp.cos(angles), jnp.sin(angles))


def rotate(value, cosine, sine_table):
    half_width = value.shape[-1] // 2
    front_half = value[..., :half_width]
    back_half = value[..., half_width:]
    return jnp.concatenate(
        [
            front_half * cosine - back_half * sine_table,
            back_half * cosine + front_half * sine_table,
        ],
        axis=-1,
    )


def silu_parts(value):
    logistic = jax.nn.sigmoid(value)
    return (value * logistic, logistic * (1.0 + value * (1.0 - logistic)))


def turn_pairs():
    pairs = []
    for e in range(N_EXPERT):
        for s in range(N_SHARD):
            pairs.append((e * N_SHARD + s, (N_SHARD * (e % 2) + s) * N_SHARD + e // 2))
    return pairs


def in_order(first, then):
    return lax.optimization_barrier((first, then))


def zero_after(*firsts):
    total = 0.0
    for first in firsts:
        tile = first.reshape(-1, first.shape[-1])[:8, :128]
        total = jnp.maximum(total, jnp.max(tile.astype(F32)))
    return jnp.where(total != total, total, 0.0)


def peek_kernel(tile_ref, before_ref, zero_ref):
    tile = tile_ref[...].astype(F32) + before_ref[0]
    zero_ref[...] = jnp.where(tile != tile, tile, 0.0)


def peek(first, before=None):
    flat = first.reshape(-1, first.shape[-1])
    if before is None:
        before = jnp.zeros((), F32)
    zeros = pl.pallas_call(
        peek_kernel,
        grid=(1,),
        in_specs=[
            pl.BlockSpec((16, 128), lambda i: (0, 0)),
            pl.BlockSpec(memory_space=pltpu.SMEM),
        ],
        out_specs=pl.BlockSpec((16, 128), lambda i: (0, 0)),
        out_shape=jax.ShapeDtypeStruct((16, 128), F32),
        cost_estimate=pl.CostEstimate(flops=4096, bytes_accessed=12288, transcendentals=0),
    )(flat, before.reshape(1))
    return zeros[:8]


def owner_grads_kernel(normed_ref, grad_ref, expand_ref, gain_ref, head_ref, latent_ref):
    acc = product_nt(normed_ref[...].T, grad_ref[...]).astype(BF)
    head_ref[0, :, :QW] = acc[:, :QW]
    head_ref[0, :, QW:] = expand_ref[0]
    gain = gain_ref[0].astype(BF)
    for s in range(N_SHARD):
        own = slice(16 * s, 16 * s + 16)
        latent_ref[s, :, :R] = acc[own, QW : QW + R]
        latent_ref[s, :, R:] = gain[own]
        latent_ref[s, :, R:LW] = acc[own, QW + R :]


def owner_grads(normed, grad, expand, gain):
    tokens = normed.shape[0]
    return pl.pallas_call(
        owner_grads_kernel,
        grid=(N_EXPERT,),
        in_specs=[
            pl.BlockSpec((tokens, 128), lambda i: (0, i)),
            pl.BlockSpec((QW + LW, tokens), lambda i: (0, 0)),
            pl.BlockSpec((1, 128, 128), lambda i: (i, 0, 0)),
            pl.BlockSpec((1, 128, 128), lambda i: (i, 0, 0)),
        ],
        out_specs=[
            pl.BlockSpec((1, 128, QW + 128), lambda i: (i, 0, 0)),
            pl.BlockSpec((N_SHARD, 16, 640), lambda i: (0, i, 0)),
        ],
        out_shape=[
            jax.ShapeDtypeStruct((N_EXPERT, 128, QW + 128), BF),
            jax.ShapeDtypeStruct((N_SHARD, N_EXPERT * 16, 640), BF),
        ],
        compiler_params=pltpu.CompilerParams(vmem_limit_bytes=24 * 1024 * 1024),
        cost_estimate=pl.CostEstimate(
            flops=2 * tokens * 2048 * 960, bytes_accessed=12 * 1024 * 1024, transcendentals=0
        ),
    )(normed, grad.T, expand, gain)


def in_turn(then, *firsts):
    return then + zero_after(*firsts).astype(then.dtype)


def sum_over_expert(pieces):
    got = lax.all_to_all(pieces, "expert", split_axis=0, concat_axis=0, tiled=True)
    return jnp.sum(got.astype(F32), axis=0)


def to_owners(pieces):
    got = lax.all_to_all(
        pieces, ("expert", "shard"), split_axis=0, concat_axis=0, tiled=True
    )
    return got.reshape((N_EXPERT, N_SHARD) + pieces.shape[1:]).astype(F32)


def body(
    hidden_in,
    cotangent,
    lengths,
    dealing,
    routes,
    norm_attn,
    w_query,
    w_latent,
    norm_latent,
    w_expand,
    w_out,
    norm_ffn,
    w_router,
    w_shared_gate,
    w_shared_up,
    w_shared_down,
    w_expert_gate,
    w_expert_up,
    w_expert_down,
):
    rows, width = hidden_in.shape
    group = rows * N_SHARD
    expert_count = EXP_DEV * N_EXPERT
    factor = (DN + DR) ** (-0.5)
    hid = w_shared_gate.shape[1] // N_SHARD
    my_shard = lax.axis_index("shard")
    my_first = my_shard * rows
    pairs = turn_pairs()
    back_pairs = [(b, a) for a, b in pairs]

    def spread(block):
        return jnp.broadcast_to(block[None], (N_SHARD,) + block.shape)

    def split_columns(block):
        return block.reshape(16, N_SHARD, -1).transpose(1, 0, 2)

    x_group = lax.all_gather(hidden_in, "shard", axis=0, tiled=True)
    latent_gain16 = jnp.pad(norm_latent, (0, 12))
    gains = jnp.stack([norm_attn, norm_ffn, latent_gain16], axis=1)
    expand_block = w_expand.reshape(4, N_SHARD, KVW // 128, 128).transpose(1, 0, 2, 3)
    columns = jnp.concatenate(
        [
            split_columns(w_query),
            spread(w_latent),
            expand_block.reshape(N_SHARD, 16, 128),
            spread(jnp.pad(gains, ((0, 0), (0, 61)))),
            spread(w_router),
            jnp.zeros((N_SHARD, 16, 64), BF),
            split_columns(w_shared_gate),
            split_columns(w_shared_up),
        ],
        axis=2,
    ).reshape(N_SHARD * 16, 1280 + 2 * hid)
    columns = lax.all_to_all(columns, "shard", split_axis=0, concat_axis=0, tiled=True)
    turned = lax.ppermute(
        jnp.concatenate([w_out, w_shared_down, jnp.zeros((5, width), BF)], axis=0),
        ("expert", "shard"),
        pairs,
    )
    weights = lax.all_gather(
        in_turn(
            jnp.concatenate([columns[:, :1280], turned[:16].reshape(128, 256)], axis=1), x_group
        ),
        "expert",
        axis=0,
        tiled=True,
    )

    place = dealing[0]
    seq_lengths = lengths[0]
    seq_ends = jnp.cumsum(seq_lengths)
    seq_starts = seq_ends - seq_lengths
    seq_ids = jnp.arange(seq_lengths.shape[0], dtype=jnp.int32)
    segment = jnp.sum((place[:, None] >= seq_ends[None, :]).astype(jnp.int32), axis=1)
    start = jnp.sum(
        jnp.where(segment[:, None] == seq_ids[None, :], seq_starts[None, :], 0), axis=1
    )
    cosine, sine = rope_tables(place - start, DR)
    allowed = (place[None, :] <= place[:, None]) & (place[None, :] >= start[:, None])

    flat_expert = routes.reshape(-1)
    earlier = jnp.arange(rows * TOPK)
    same = (flat_expert[:, None] == flat_expert[None, :]) & (earlier[None, :] < earlier[:, None])
    rank = jnp.sum(same.astype(jnp.int32), axis=1)
    slot = (
        (flat_expert // EXP_DEV) * SLOT + (flat_expert % EXP_DEV) * CAP + rank
    ).reshape(rows, TOPK)
    slot_ids = jnp.arange(N_EXPERT * SLOT, dtype=jnp.int32)
    hot = [(slot[:, k][:, None] == slot_ids[None, :]) for k in range(TOPK)]
    hot_any = (hot[0] | hot[1]).astype(BF)
    own_rows = EXP_DEV * N_EXPERT * CAP
    ids = jnp.arange(own_rows, dtype=jnp.int32)
    by_source = (
        (ids % (N_EXPERT * CAP)) // CAP * SLOT + ids // (N_EXPERT * CAP) * CAP + ids % CAP
    )
    deal = (by_source[:, None] == slot_ids[None, :]).astype(BF)

    def to_owner(packed):
        arrived = lax.all_to_all(packed, "expert", split_axis=0, concat_axis=0, tiled=True)
        return product(deal, arrived).astype(BF).reshape(EXP_DEV, N_EXPERT * CAP, width)

    def from_owner(own):
        packed = product_tn(deal, own.reshape(own_rows, width)).astype(BF)
        return lax.all_to_all(packed, "expert", split_axis=0, concat_axis=0, tiled=True)

    own_cot = to_owner(product_tn(hot_any, in_turn(cotangent, columns)).astype(BF))
    weights, own_cot = in_order(weights, own_cot)
    expert_cot = lax.all_gather(own_cot, "shard", axis=1, tiled=True)
    query_latent_w = weights[:, : QW + LW]
    query_w = weights[:, :QW]
    latent_w = weights[:, QW : QW + LW]
    expand_w = weights[:, 960:1088].reshape(R, KVW)
    gain_attn = weights[:, 1088].astype(F32)
    gain_ffn = weights[:, 1089].astype(F32)
    gain_latent = weights[:, 1090].reshape(128, 16)[:, :4].reshape(R).astype(F32)
    router_w = weights[:, 1152 : 1152 + expert_count]
    out_w = weights[:, 1280:].reshape(N_EXPERT * 16, width)

    ffn_sent = jnp.concatenate([columns[:, 1280:], turned[16:27].reshape(128, hid)], axis=1)
    ffn_sent = jnp.broadcast_to(
        in_turn(ffn_sent, weights)[None], (N_EXPERT,) + ffn_sent.shape
    ).reshape(N_EXPERT * 128, 3 * hid)
    ffn_w = lax.all_to_all(ffn_sent, "expert", split_axis=0, concat_axis=0, tiled=True)
    gate_up_w = ffn_w[:, : 2 * hid]
    down_w = ffn_w[:, 2 * hid :].reshape(hid, width)

    x_all = x_group.astype(F32)
    normed_f, _ = rms_forward(x_all, gain_attn)
    normed_in = normed_f.astype(BF)
    projected = product(normed_in, query_latent_w)
    compressed = projected[:, QW : QW + R]
    latent_f, _ = rms_forward(compressed, gain_latent)
    latent_normed = latent_f.astype(BF)
    expanded = product(latent_normed, expand_w).astype(BF)
    key_rope = rotate(projected[:, QW + R :], cosine, sine).astype(BF)
    queries = []
    keys = []
    values = []
    for h in range(HEADS):
        q_h = projected[:, h * (DN + DR) : (h + 1) * (DN + DR)]
        queries.append(
            jnp.concatenate([q_h[:, :DN], rotate(q_h[:, DN:], cosine, sine)], axis=1).astype(BF)
        )
        kv_h = expanded[:, h * (DN + DV) : (h + 1) * (DN + DV)]
        keys.append(jnp.concatenate([kv_h[:, :DN], key_rope], axis=1))
        values.append(kv_h[:, DN:])
    probs_low = []
    mixed = []
    for h in range(HEADS):
        masked = jnp.where(allowed, product_nt(queries[h], keys[h]) * factor, MASKED)
        peak = jnp.max(masked, axis=-1, keepdims=True)
        raised = jnp.exp(masked - peak)
        probs = raised / jnp.sum(raised, axis=-1, keepdims=True)
        probs_low.append(probs.astype(BF))
        mixed.append(product(probs_low[h], values[h]))
    attended = jnp.concatenate(mixed, axis=1).astype(BF)
    attended = in_turn(attended, peek(expert_cot), ffn_w)
    out_part = product(attended, out_w).astype(BF)
    out_own = lax.psum_scatter(out_part, "shard", scatter_dimension=0, tiled=True)
    w_expert_both = jnp.concatenate([w_expert_gate, w_expert_up], axis=1)
    out_own = in_turn(out_own, peek(w_expert_both))
    inputs32 = hidden_in.astype(F32)
    middle = inputs32 + out_own.astype(F32)
    mid_f, inverse_mid = rms_forward(middle, gain_ffn)
    normed_mid = mid_f.astype(BF)

    logits = product(normed_mid, router_w)
    route_hot = (
        routes[:, :, None] == jnp.arange(expert_count, dtype=jnp.int32)[None, None, :]
    ).astype(F32)
    chosen = jnp.sum(route_hot * logits[:, None, :], axis=-1)
    scores_sig = jax.nn.sigmoid(chosen)
    sig_total = jnp.sum(scores_sig, axis=1, keepdims=True)
    gate_values = ROUTE_SCALE * scores_sig / sig_total
    slot_gate = sum(
        jnp.sum(jnp.where(hot[k], gate_values[:, k][:, None], 0.0), axis=0) for k in range(TOPK)
    )

    own_sent = to_owner(product_tn(hot_any, normed_mid).astype(BF))
    mid_group = lax.all_gather(normed_mid, "shard", axis=0, tiled=True)
    mid_group, own_sent = in_order(mid_group, own_sent)
    expert_rows = lax.all_gather(own_sent, "shard", axis=1, tiled=True)
    gate_rows = jnp.broadcast_to(
        slot_gate.reshape(N_EXPERT, 1, SLOT)[:, :, : EXP_DEV * CAP],
        (N_EXPERT, N_SHARD, EXP_DEV * CAP),
    ).reshape(N_EXPERT * N_SHARD, EXP_DEV * CAP)
    gate_rows = lax.all_to_all(
        gate_rows, ("expert", "shard"), split_axis=0, concat_axis=0, tiled=True
    )
    gate_rows = (
        gate_rows.reshape(N_EXPERT, N_SHARD, EXP_DEV, CAP)
        .transpose(2, 1, 0, 3)
        .reshape(EXP_DEV, N_SHARD * N_EXPERT * CAP, 1)
    )

    mid_sent = in_turn(mid_group, gate_rows)
    shared_ab = product(mid_sent, gate_up_w)
    shared_a = shared_ab[:, :hid]
    shared_b = shared_ab[:, hid:]
    silu_shared, slope_shared = silu_parts(shared_a)
    shared_hidden = (silu_shared * shared_b).astype(BF)
    shared_part = product(shared_hidden, down_w).astype(BF)
    expert_first, cot_sent = in_order(
        zero_after(peek(expert_rows, zero_after(gate_rows, shared_part))), cotangent
    )
    cot_group = lax.all_gather(cot_sent, "shard", axis=0, tiled=True)

    both_pre = jnp.einsum("jsd,jfd->jsf", expert_rows, w_expert_both, preferred_element_type=F32)
    gate_pre = both_pre[..., :hid]
    up_pre = both_pre[..., hid:]
    silu_gate, slope_gate = silu_parts(gate_pre)
    expert_hidden = (silu_gate * up_pre).astype(BF)
    expert_hidden = expert_hidden + expert_first.astype(BF)
    hidden_grad = gate_rows * jnp.einsum(
        "jsd,jfd->jsf", expert_cot, w_expert_down, preferred_element_type=F32
    )
    gate_part = jnp.sum(expert_hidden.astype(F32) * hidden_grad, axis=-1)
    grad_gate_pre = (hidden_grad * up_pre * slope_gate).astype(BF)
    grad_up_pre = (hidden_grad * silu_gate).astype(BF)
    row_part = jnp.einsum(
        "jsf,jfd->jsd",
        jnp.concatenate([grad_gate_pre, grad_up_pre], axis=2),
        w_expert_both,
        preferred_element_type=F32,
    ).astype(BF)
    row_own = lax.psum_scatter(row_part, "shard", scatter_dimension=1, tiled=True)
    gate_sent = (
        gate_part.reshape(EXP_DEV, N_SHARD, N_EXPERT, CAP)
        .transpose(2, 1, 0, 3)
        .reshape(N_EXPERT * N_SHARD, EXP_DEV * CAP)
    )
    gate_got = lax.all_to_all(
        gate_sent, ("expert", "shard"), split_axis=0, concat_axis=0, tiled=True
    )
    gate_sum = jnp.sum(gate_got.reshape(N_EXPERT, N_SHARD, EXP_DEV * CAP), axis=1)
    gate_slots = jnp.pad(gate_sum, ((0, 0), (0, SLOT - EXP_DEV * CAP))).reshape(-1)
    gate_times_grad = jnp.stack(
        [jnp.sum(jnp.where(hot[k], gate_slots[None, :], 0.0), axis=1) for k in range(TOPK)], axis=1
    )

    gate_total = jnp.sum(gate_times_grad, axis=1, keepdims=True)
    chosen_grad = (gate_times_grad - gate_values * (gate_total / ROUTE_SCALE)) * (
        1.0 - scores_sig
    )
    logit_grad = jnp.sum(route_hot * chosen_grad[:, :, None], axis=1).astype(BF)

    shared_hidden_grad = product_nt(cot_group, down_w)
    grad_shared_ab = jnp.concatenate(
        [shared_hidden_grad * shared_b * slope_shared, shared_hidden_grad * silu_shared], axis=1
    ).astype(BF)
    shared_row_part = product_nt(grad_shared_ab, gate_up_w).astype(BF)
    gate_up_sum = sum_over_expert(
        jnp.concatenate(
            [
                product_tn(mid_sent, grad_shared_ab).astype(BF),
                product_tn(normed_mid, logit_grad).astype(BF),
            ],
            axis=1,
        ).reshape(N_EXPERT, 128, 2 * hid + expert_count)
    )
    row_own = in_turn(row_own, gate_got, gate_up_sum)
    row_own, shared_row_part = in_order(row_own, shared_row_part)
    shared_row = lax.psum_scatter(shared_row_part, "shard", scatter_dimension=0, tiled=True)
    row_back = from_owner(row_own)

    grad_routes = product(hot_any.astype(BF), row_back)
    grad_top = cotangent.astype(F32)
    normed_grad = product_nt(logit_grad, router_w) + shared_row.astype(F32) + grad_routes
    middle_norm_grad, grad_gain_ffn = rms_backward(middle, inverse_mid, gain_ffn, normed_grad)
    middle_grad = grad_top + middle_norm_grad
    attn_grad = middle_grad.astype(BF)
    grad_group = lax.all_gather(attn_grad, "shard", axis=0, tiled=True)
    ffn_got = lax.all_to_all(
        in_turn(gate_up_sum, attn_grad).astype(BF),
        "shard",
        split_axis=0,
        concat_axis=0,
        tiled=True,
    )
    ffn_got = ffn_got.reshape(N_SHARD, 16, 2 * hid + expert_count).astype(F32)
    expert_part = jnp.einsum(
        "jsf,jfd->jsd",
        in_turn(expert_hidden, attn_grad),
        w_expert_down,
        preferred_element_type=F32,
    ).astype(BF)
    expert_own = lax.psum_scatter(expert_part, "shard", scatter_dimension=1, tiled=True)
    mixed = [in_turn(one, expert_part, ffn_got) for one in mixed]

    attended_grad = product_nt(grad_group, out_w).astype(BF)
    out_sum = sum_over_expert(
        product_tn(attended, grad_group)
        .astype(BF)
        .reshape(N_EXPERT, 16, width)
    )
    query_grads = []
    expanded_grads = []
    rope_grad = 0.0
    for h in range(HEADS):
        a_h = attended_grad[:, h * DV : (h + 1) * DV]
        inner = in_turn(jnp.sum(mixed[h] * a_h.astype(F32), axis=-1, keepdims=True), out_sum)
        probs_grad = product_nt(a_h, values[h])
        score_grad = (probs_low[h].astype(F32) * (probs_grad - inner)).astype(BF)
        value_grad = product_tn(probs_low[h], a_h)
        query_grad = product(score_grad, keys[h]) * factor
        key_grad = product_tn(score_grad, queries[h]) * factor
        query_grads.append(query_grad[:, :DN])
        query_grads.append(rotate(query_grad[:, DN:], cosine, -sine))
        expanded_grads.append(key_grad[:, :DN])
        expanded_grads.append(value_grad)
        rope_grad = rope_grad + key_grad[:, DN:]
    down_sum = sum_over_expert(
        jnp.pad(
            product_tn(in_turn(shared_hidden, out_sum, rope_grad), cot_group)
            .astype(BF)
            .reshape(N_EXPERT, 11, width),
            ((0, 0), (0, 5), (0, 0)),
        )
    )
    expanded_grad = jnp.concatenate(expanded_grads, axis=1).astype(BF)
    inverse_latent = lax.rsqrt(
        jnp.mean(compressed * compressed, axis=-1, keepdims=True) + EPSILON
    )
    compressed_grad, _ = rms_backward(
        compressed, inverse_latent, gain_latent, product_nt(expanded_grad, expand_w)
    )
    projected_grad = jnp.concatenate(
        query_grads + [compressed_grad, rotate(rope_grad, cosine, -sine)], axis=1
    ).astype(BF)

    ffn_gain = jnp.pad(grad_gain_ffn.reshape(N_EXPERT, 128, 1), ((0, 0), (0, 0), (64, 63)))
    normed_part = product_nt(projected_grad, query_latent_w).astype(BF)
    expert_own, normed_part = in_order(expert_own, normed_part)
    normed_in_grad = lax.psum_scatter(normed_part, "shard", scatter_dimension=0, tiled=True)
    grads_sent, latent_sent = owner_grads(
        normed_in,
        projected_grad,
        product_tn(latent_normed, expanded_grad).astype(BF).reshape(N_EXPERT, 128, 128),
        in_turn(ffn_gain, normed_part, down_sum),
    )
    grads_sum = sum_over_expert(grads_sent)
    latent_own = lax.psum_scatter(
        latent_sent.reshape(N_SHARD * N_EXPERT * 16, 640),
        "shard",
        scatter_dimension=0,
        tiled=True,
    )
    normed_in_grad, shared_part = in_order(normed_in_grad, shared_part)
    shared_out = lax.psum_scatter(shared_part, "shard", scatter_dimension=0, tiled=True)
    grads_got = lax.all_to_all(
        grads_sum.astype(BF), "shard", split_axis=0, concat_axis=0, tiled=True
    )
    grads_got = grads_got.reshape(N_SHARD, 16, QW + 128).astype(F32)
    latent_sum = sum_over_expert(latent_own.reshape(N_EXPERT, 16, 640))
    turned_back = lax.ppermute(
        in_turn(jnp.concatenate([out_sum, down_sum], axis=0), grads_sum).astype(BF),
        ("expert", "shard"),
        back_pairs,
    ).astype(F32)

    grad_expert_down = jnp.einsum(
        "jsf,jsd->jfd",
        in_turn((expert_hidden.astype(F32) * gate_rows).astype(BF), grads_sent),
        expert_cot,
        preferred_element_type=F32,
    )
    grad_expert_gate = jnp.einsum(
        "jsf,jsd->jfd",
        in_turn(grad_gate_pre, grads_sent),
        expert_rows,
        preferred_element_type=F32,
    )
    grad_expert_up = jnp.einsum(
        "jsf,jsd->jfd",
        in_turn(grad_up_pre, grads_sent),
        expert_rows,
        preferred_element_type=F32,
    )

    normed_in_grad = normed_in_grad.astype(F32)
    inverse_in = lax.rsqrt(jnp.mean(inputs32 * inputs32, axis=-1, keepdims=True) + EPSILON)
    input_norm_grad, _ = rms_backward(
        inputs32, inverse_in, gain_attn, normed_in_grad
    )
    grad_input = middle_grad + input_norm_grad

    expert_back = from_owner(expert_own)
    route_out = [product(hot[k].astype(BF), expert_back) for k in range(TOPK)]
    mixture = sum(gate_values[:, k][:, None] * route_out[k] for k in range(TOPK))
    layer_out = (middle + shared_out.astype(F32) + mixture).astype(BF)

    grad_shared_gate = ffn_got[:, :, :hid].transpose(1, 0, 2).reshape(16, N_SHARD * hid)
    grad_shared_up = (
        ffn_got[:, :, hid : 2 * hid].transpose(1, 0, 2).reshape(16, N_SHARD * hid)
    )
    grad_router_own = jnp.sum(ffn_got[:, :, 2 * hid :], axis=0)
    grad_shared_down = turned_back[16:27]
    grad_out_own = turned_back[:16]

    query_own = grads_got[:, :, :QW].transpose(1, 0, 2).reshape(16, N_SHARD * QW)
    grad_expand_own = (
        grads_got[:, :, QW : QW + 128]
        .reshape(N_SHARD, 4, KVW // 128, 128)
        .transpose(1, 0, 2, 3)
        .reshape(4, N_SHARD * KVW)
    )
    grad_latent_own = latent_sum[:, :LW]
    grad_norm_ffn = latent_sum[:, LW]
    grad_norm_attn = (
        jnp.sum(w_query.astype(F32) * query_own, axis=1)
        + jnp.sum(w_latent.astype(F32) * grad_latent_own, axis=1)
    ) / norm_attn.astype(F32)
    grad_norm_latent = jnp.sum(w_expand.astype(F32) * grad_expand_own, axis=1) / (
        norm_latent.astype(F32)
    )

    return (
        layer_out,
        grad_input,
        grad_norm_attn,
        query_own,
        grad_latent_own,
        grad_norm_latent,
        grad_expand_own,
        grad_out_own,
        grad_norm_ffn,
        grad_router_own,
        grad_shared_gate,
        grad_shared_up,
        grad_shared_down,
        grad_expert_gate,
        grad_expert_up,
        grad_expert_down,
    )


def solution(mesh):
    both = P(("expert", "shard"), None)
    vector = P(("expert", "shard"))
    groups = P("expert", None)
    experts = P("expert", "shard", None)
    return jax.shard_map(
        body,
        mesh=mesh,
        in_specs=(
            both,
            both,
            groups,
            groups,
            both,
            vector,
            both,
            both,
            vector,
            both,
            both,
            vector,
            both,
            both,
            both,
            both,
            experts,
            experts,
            experts,
        ),
        out_specs=(
            both,
            both,
            vector,
            both,
            both,
            vector,
            both,
            both,
            vector,
            both,
            both,
            both,
            both,
            experts,
            experts,
            experts,
        ),
        check_vma=False,
    )
```

time: 4930 us -> 774 us (0.16)
  waiting for transfers between devices: 3530 us -> 247 us
  blocking collectives: 614 us -> 47.6 us
  local copies, waits for them, and re-layouts: 282 us -> 91.8 us
  starting transfers between devices: 196 us -> 88.2 us
  matrix products: 241 us -> 166 us
    reduce_scatter x8 -> x7, waiting for transfers between devices: 2970 us -> 55.8 us  [the longest x1 25 us: body(): lax.psum_scatter(out_part, 'shard', scatter_dimension=0, tiled=True)]
    unnamed x3 -> x0, blocking collectives: 515 us -> none
    all_gather x10 -> x7, waiting for transfers between devices: 466 us -> 73.4 us  [the longest x1 30 us: body(): lax.all_gather(in_turn(jnp.concatenate([columns[:, :1280], turned[:16].re...]
    unnamed x43 -> x0, starting transfers between devices: 180 us -> none
    unnamed x239 -> x267, local copies, waits for them, and re-layouts: 134 us -> 30.5 us
    scatter x4 -> x0, local copies, waits for them, and re-layouts: 97.3 us -> none  [pack(): return buffer.at[flat_local, send_column].set(rows_flat)]
    all_to_all x2 -> x13, waiting for transfers between devices: 16 us -> 105 us  [the longest x5 47.2 us: sum_over_expert(): lax.all_to_all(pieces, 'expert', split_axis=0, concat_axis=0, tiled=True)]
    unnamed x64 -> x14, waiting for transfers between devices: 78.6 us -> 1.38 us
  transfers between devices with their start and end apart: 63 -> 29, of which waited for: 24 -> 19; matrix products, arithmetic and copies ran while one was open for 14% -> 37% of each run, Pallas kernels for 0% -> 2%
where the time goes in v1:
time: 774 us; the launch traced here: 764 us
  waiting for transfers between devices  247 us (32%)
  matrix products  166 us (21%)
  local copies, waits for them, and re-layouts  91.8 us (12%)
  starting transfers between devices  88.2 us (11%)
  other arithmetic  76 us (10%)
  blocking collectives  47.6 us (6%)
  between operations  29.3 us (4%)
  Pallas kernels  17.8 us (2%)
    all_to_all x5, waiting for transfers between devices, sum_over_expert(): lax.all_to_all(pieces, 'expert', split_axis=0, concat_axis=0, tiled=True)  47.2 us
    dot_general x15, matrix products, product(): return jnp.dot(left, right, preferred_element_type=F32)  41.4 us
    dot_general x10, matrix products, product_nt(): lax.dot_general(left, right, (((1,), (1,)), ((), ())), preferred_element_...  31.9 us
    all_to_all x5, starting transfers between devices, sum_over_expert(): lax.all_to_all(pieces, 'expert', split_axis=0, concat_axis=0, tiled=True)  31.8 us
    unnamed x267, local copies, waits for them, and re-layouts  30.5 us
    all_gather x1, waiting for transfers between devices, body(): lax.all_gather(in_turn(jnp.concatenate([columns[:, :1280], turned[:16].re...  30 us
    all_to_all x1, blocking collectives, to_owner(): lax.all_to_all(packed, 'expert', split_axis=0, concat_axis=0, tiled=True)  29.8 us
    all_to_all x1, waiting for transfers between devices, to_owner(): lax.all_to_all(packed, 'expert', split_axis=0, concat_axis=0, tiled=True)  29.6 us
  transfers between devices with their start and end apart: 29, of which 19 were waited for; matrix products, arithmetic and copies ran while one was open for 37% of the time, Pallas kernels for 2%

profile of v1, /device:TPU:8, one launch (start us, length us, event | category | flops | bytes accessed | tf_op | source)
XLA Modules:
  0.0 764.4 jit_solution(9996377296705612585)
XLA Ops:
  15.6 5.0 all-to-all-start
  20.8 5.3 collective-permute-start
  26.1 11.9 %collective-permute-done = bf16[32,2048]{1,0:T(8,128)(2,1)S(1)} collective-permute-done((bf16[32,2048]{1,0:T(8,128)(2,1)S(1)}, bf16[32,2048]{1,0:T(8,128)(2,1)S(1)}, u32[]{:S(2)}, u32[]{:S(2)}) %collective-permute-start) | collective-permute-done | bytes 131104 | tf_op jit(solution)/shard_map/ppermute | solution.py:233
  40.4 11.6 %all-gather.8.cloned.1.call-done = bf16[1024,2048]{1,0:T(8,128)(2,1)} async-done(((bf16[128,2048]{1,0:T(8,128)(2,1)}), bf16[1024,2048]{1,0:T(8,128)(2,1)}) %all-gather.8.cloned.1.call-update) | async-done | bytes 4194320 | tf_op jit(solution)/shard_map/all_gather | solution.py:215
  61.8 7.5 all-to-all-start.1
  69.4 29.6 %all-to-all-done.1 = bf16[16,24,2048]{2,1,0:T(8,128)(2,1)} async-done(((bf16[16,24,2048]{2,1,0:T(8,128)(2,1)}), bf16[16,24,2048]{2,1,0:T(8,128)(2,1)}, u32[]{:S(2)}, u32[]{:S(2)}) %all-to-all-start.1) | async-done | bytes 1572896 | tf_op jit(solution)/shard_map/all_to_all | solution.py:277
  102.3 30.0 %all-gather.10.cloned.1.call-done = bf16[2048,1536]{1,0:T(8,128)(2,1)} async-done(((bf16[128,1536]{1,0:T(8,128)(2,1)}), bf16[2048,1536]{1,0:T(8,128)(2,1)}) %all-gather.10.cloned.1.call-update) | async-done | bytes 6291472 | tf_op jit(solution)/shard_map/all_gather | solution.py:238
  153.1 5.3 all-to-all-start.2
  164.0 8.1 %fusion.190 = (bf16[1024,960]{0,1:T(8,128)(2,1)S(1)}, f32[1024,960]{0,1:T(8,128)S(1)}) fusion(bf16[1024,2048]{1,0:T(8,128)(2,1)S(1)} %fusion.2.normed_ref, bf16[2048,1536]{1,0:T(8,128)(2,1)} %all-gather.10.cloned.1.call-done), kind=kOutput, calls=%fused_computation.376 | convolution fusion | flops 4027514880 | bytes 14286848 | tf_op jit(solution)/shard_map/dot_general | solution.py:33
  197.4 4.5 convolution_convert_fusion.4
  210.9 25.0 %reduce-scatter.8.cloned.1.call-done = bf16[128,2048]{1,0:T(8,128)(2,1)} async-done(((bf16[1024,2048]{1,0:T(8,128)(2,1)}), bf16[128,2048]{1,0:T(8,128)(2,1)}) %reduce-scatter.8.cloned.1.call-update) | async-done | bytes 524304 | tf_op jit(solution)/shard_map/reduce_scatter | solution.py:337
  241.8 29.8 %all_to_all.121 = bf16[16,24,2048]{2,1,0:T(8,128)(2,1)S(1)} all-to-all(bf16[16,24,2048]{2,1,0:T(8,128)(2,1)S(1)} %bitcast.152), channel_id=1, replica_groups=mesh['expert'=16,'shard'=8] {'expert'}, dimensions={0} | all-to-all | bytes 3145728 | tf_op jit(solution)/shard_map/all_to_all | solution.py:277
  277.2 9.1 %all-to-all-start.4 = ((f32[128,1,20]{2,1,0:T(1,128)}), f32[128,1,20]{2,1,0:T(1,128)S(1)}, u32[]{:S(2)}, u32[]{:S(2)}) async-start(f32[128,1,20]{2,1,0:T(1,128)} %bitcast.27), calls=%async_computation.5 | async-start | bytes 131072 | tf_op jit(solution)/shard_map/all_to_all | solution.py:365
  290.8 4.5 reshape.492
  300.7 4.4 fusion.7
  312.6 22.3 %all-gather.16.cloned.1.call-done = bf16[4,640,2048]{2,1,0:T(8,128)(2,1)} async-done(((bf16[4,80,2048]{2,1,0:T(8,128)(2,1)}), bf16[4,640,2048]{2,1,0:T(8,128)(2,1)}) %all-gather.16.cloned.1.call-update) | async-done | bytes 10485776 | tf_op jit(solution)/shard_map/all_gather | solution.py:360
  339.6 12.1 %fusion.195 = f32[4,640,352]{1,2,0:T(8,128)} fusion(bf16[4,640,2048]{2,1,0:T(8,128)(2,1)} %all-gather.16.cloned.1.call-done, bf16[4,352,2048]{2,1,0:T(8,128)(2,1)} %copy-done.15), kind=kOutput, calls=%fused_computation.381 | convolution fusion | flops 3690987520 | bytes 19857408 | tf_op jit(solution)/shard_map/jsd,jfd->jsf/dot_general | solution.py:386
  351.7 10.7 %fusion.20 = (f32[4,640]{1,0:T(4,128)S(1)}, bf16[4,640,176]{1,2,0:T(8,128)(2,1)}, bf16[4,640,176]{1,2,0:T(8,128)(2,1)}, bf16[4,640,176]{1,2,0:T(8,128)(2,1)}) fusion(f32[4,640]{1,0:T(4,128)S(1)} %mul.555, bf16[]{:T(256)S(6)} %select_n.169, f32[4,640,352]{1,2,0:T(8,128)} %fusion.195, bf16[4,640,2048]{2,1,0:T(8,128)(2,1)} %all-gather.12.cloned.1.call-done, ...), kind=kOutput, calls=%fused_computation.63 | convolution fusion | flops 1854502400 | bytes 19697666 | tf_op jit(solution)/shard_map/jsd,jfd->jsf/dot_general | solution.py:392
  362.4 10.7 %convolution_convert_fusion.1 = bf16[4,640,2048]{2,1,0:T(8,128)(2,1)} fusion(bf16[4,352,2048]{2,1,0:T(8,128)(2,1)} %copy-done.15, bf16[4,640,176]{1,2,0:T(8,128)(2,1)} %get-tuple-element.62, bf16[4,640,176]{1,2,0:T(8,128)(2,1)} %get-tuple-element.61), kind=kOutput, calls=%fused_computation.6 | convolution fusion | flops 3699834880 | bytes 18055168 | tf_op jit(solution)/shard_map/jsf,jfd->jsd/dot_general | solution.py:398
  377.2 17.8 %all_to_all.122 = f32[128,1,20]{2,1,0:T(1,128)S(1)} all-to-all(f32[128,1,20]{2,1,0:T(1,128)S(1)} %copy.230), channel_id=1, replica_groups=mesh['expert'=16,'shard'=8] {'expert','shard'}, dimensions={0} | all-to-all | bytes 20480 | tf_op jit(solution)/shard_map/all_to_all | solution.py:410
  399.4 4.8 multiply_convert_fusion.8
  407.4 4.4 all-to-all-start.6
  413.1 6.1 convolution_convert_fusion.2
  419.2 18.3 %all-to-all-done.6 = bf16[16,128,416]{1,2,0:T(8,128)(2,1)} async-done(((bf16[16,128,416]{1,2,0:T(8,128)(2,1)}), bf16[16,128,416]{1,2,0:T(8,128)(2,1)}, u32[]{:S(2)}, u32[]{:S(2)}) %all-to-all-start.6) | async-done | bytes 1703968 | tf_op jit(solution)/shard_map/all_to_all | solution.py:167
  447.9 4.6 all-to-all-start.7
  452.5 23.7 %reduce-scatter.12.cloned.1.call-done = bf16[128,2048]{1,0:T(8,128)(2,1)} async-done(((bf16[1024,2048]{1,0:T(8,128)(2,1)}), bf16[128,2048]{1,0:T(8,128)(2,1)}) %reduce-scatter.12.cloned.1.call-update) | async-done | bytes 524304 | tf_op jit(solution)/shard_map/reduce_scatter | solution.py:441
  486.3 6.7 convolution_convert_fusion
  494.8 7.8 %all-to-all-start.8 = ((bf16[8,16,416]{2,1,0:T(8,128)(2,1)}), bf16[8,16,416]{2,1,0:T(8,128)(2,1)S(1)}, u32[]{:S(2)}, u32[]{:S(2)}) async-start(bf16[8,16,416]{2,1,0:T(8,128)(2,1)} %bitcast.38), calls=%async_computation.12 | async-start | bytes 262144 | tf_op jit(solution)/shard_map/all_to_all | solution.py:451
  504.5 4.5 all-to-all-done.8
  510.2 9.3 %all-gather.20.cloned.1.call-done = bf16[1024,2048]{1,0:T(8,128)(2,1)} async-done(((bf16[128,2048]{1,0:T(8,128)(2,1)}), bf16[1024,2048]{1,0:T(8,128)(2,1)}) %all-gather.20.cloned.1.call-update) | async-done | bytes 4194320 | tf_op jit(solution)/shard_map/all_gather | solution.py:450
  519.5 4.5 convolution_convert_fusion.12
  524.0 7.4 all-to-all-start.9
  531.5 4.3 convolution_convert_fusion.17
  538.5 11.2 %all-to-all-done.9 = bf16[16,16,2048]{2,1,0:T(8,128)(2,1)} async-done(((bf16[16,16,2048]{2,1,0:T(8,128)(2,1)}), bf16[16,16,2048]{2,1,0:T(8,128)(2,1)}, u32[]{:S(2)}, u32[]{:S(2)}) %all-to-all-start.9) | async-done | bytes 1048608 | tf_op jit(solution)/shard_map/all_to_all | solution.py:167
  568.2 6.3 convolution_convert_fusion.5
  575.8 7.1 reduce-scatter.14.cloned.1.call-done
  584.2 4.0 convolution_convert_fusion.13
  592.9 7.4 all-to-all-start.11
  606.3 13.6 %all-to-all-done.11 = bf16[16,16,2048]{2,1,0:T(8,128)(2,1)} async-done(((bf16[16,16,2048]{2,1,0:T(8,128)(2,1)}), bf16[16,16,2048]{2,1,0:T(8,128)(2,1)}, u32[]{:S(2)}, u32[]{:S(2)}) %all-to-all-start.11) | async-done | bytes 1048608 | tf_op jit(solution)/shard_map/all_to_all | solution.py:167
  629.2 13.9 %shard_map.309 = (bf16[16,128,512]{2,1,0:T(8,128)(2,1)S(1)}, bf16[8,256,640]{2,1,0:T(8,128)(2,1)S(1)}) custom-call(bf16[1024,2048]{1,0:T(8,128)(2,1)S(1)} %copy-done.2, bf16[960,1024]{1,0:T(8,128)(2,1)S(1)} %bitcast.144, bf16[16,128,128]{2,1,0:T(8,128)(2,1)S(1)} %reshape.501.expand_ref, f32[16,128,128]{2,1,0:T(8,128)S(1)} %pad_add_fusion.gain_ref), custom_call_target="tpu_custom_call" | custom-call | flops 4026531840 | bytes 12582912 | tf_op jit(solution)/shard_map/pallas_call | solution.py:138
  650.2 4.5 all-to-all-start.10
  659.8 19.1 %all-to-all-done.10 = bf16[16,24,2048]{2,1,0:T(8,128)(2,1)} async-done(((bf16[16,24,2048]{2,1,0:T(8,128)(2,1)}), bf16[16,24,2048]{2,1,0:T(8,128)(2,1)}, u32[]{:S(2)}, u32[]{:S(2)}) %all-to-all-start.10) | async-done | bytes 1572896 | tf_op jit(solution)/shard_map/all_to_all | solution.py:282
  678.9 4.6 all-to-all-start.12
  683.6 9.4 %fusion.40 = f32[4,176,2048]{2,1,0:T(8,128)} fusion(bf16[4,640,2048]{2,1,0:T(8,128)(2,1)} %all-gather.16.cloned.1.call-done, bf16[4,640,176]{1,2,0:T(8,128)(2,1)} %get-tuple-element.61, bf16[]{:T(256)S(6)} %select_n.179), kind=kOutput, calls=%fused_computation.107 | convolution fusion | flops 1845944320 | bytes 17154050 | tf_op jit(solution)/shard_map/jsf,jsd->jfd/dot_general | solution.py:545
  692.9 9.2 %fusion.38 = f32[4,176,2048]{2,1,0:T(8,128)} fusion(bf16[4,640,2048]{2,1,0:T(8,128)(2,1)} %all-gather.16.cloned.1.call-done, bf16[4,640,176]{1,2,0:T(8,128)(2,1)S(1)} %copy-done.40, bf16[]{:T(256)S(6)} %select_n.179), kind=kOutput, calls=%fused_computation.105 | convolution fusion | flops 1845944320 | bytes 17154050 | tf_op jit(solution)/shard_map/jsf,jsd->jfd/dot_general | solution.py:551
  702.2 5.0 fusion.36
  715.3 4.3 all-to-all-start.13
  728.2 8.0 %all-to-all-start.14 = ((bf16[16,16,640]{2,1,0:T(8,128)(2,1)}), bf16[16,16,640]{2,1,0:T(8,128)(2,1)}, u32[]{:S(2)}, u32[]{:S(2)}) async-start(bf16[16,16,640]{2,1,0:T(8,128)(2,1)} %bitcast.169), calls=%async_computation.21 | async-start | bytes 655360 | tf_op jit(solution)/shard_map/all_to_all | solution.py:167
  (520 shorter events, 236.0 us)
Async XLA Ops:
  7.2 344.5 %copy-start = (bf16[4,176,2048]{2,1,0:T(8,128)(2,1)S(1)}, bf16[4,176,2048]{2,1,0:T(8,128)(2,1)}, u32[]{:S(2)}) copy-start(bf16[4,176,2048]{2,1,0:T(8,128)(2,1)} %param.37) | copy-start | bytes 8650756
  7.2 44.8 %all-gather.8.cloned.1.call-start = ((), (), s32[]{:S(2)}) async-start(), calls=%async_computation.22 | async-start | bytes 4718592 | tf_op jit(solution)/shard_map/all_gather | solution.py:215
  14.6 41.2 %copy-start.95 = (s32[128,2]{0,1:T(2,128)S(1)}, s32[128,2]{0,1:T(2,128)}, u32[]{:S(2)}) copy-start(s32[128,2]{0,1:T(2,128)} %param.23) | copy-start | bytes 3076
  15.5 44.4 %copy-start.18 = (bf16[128,2048]{1,0:T(8,128)(2,1)S(1)}, bf16[128,2048]{1,0:T(8,128)(2,1)}, u32[]{:S(2)}) copy-start(bf16[128,2048]{1,0:T(8,128)(2,1)} %param.20) | copy-start | bytes 1572868
  15.6 23.1 %all-to-all-start = ((bf16[8,16,1632]{2,1,0:T(8,128)(2,1)}), bf16[8,16,1632]{2,1,0:T(8,128)(2,1)}, u32[]{:S(2)}, u32[]{:S(2)}) async-start(bf16[8,16,1632]{2,1,0:T(8,128)(2,1)} %concatenate.73), calls=%async_computation | async-start | bytes 851968 | tf_op jit(solution)/shard_map/all_to_all | solution.py:232
  20.6 111.7 %all-gather.10.cloned.1.call-start = ((), (), s32[]{:S(2)}) async-start(), calls=%async_computation.23 | async-start | bytes 6684672 | tf_op jit(solution)/shard_map/all_gather | solution.py:238
  20.8 17.2 %collective-permute-start = (bf16[32,2048]{1,0:T(8,128)(2,1)S(1)}, bf16[32,2048]{1,0:T(8,128)(2,1)S(1)}, u32[]{:S(2)}, u32[]{:S(2)}) collective-permute-start(bf16[32,2048]{1,0:T(8,128)(2,1)S(1)} %maximum_maximum_fusion), channel_id=1, source_target_pairs={{0,0},{1,8},{2,16},{3,24},{4,32},{5,40},{6,48},{7,56},{8,64},{9,72... | collective-permute-start | bytes 393224 | tf_op jit(solution)/shard_map/ppermute | solution.py:233
  58.0 217.8 %copy-start.85 = (s32[128]{0:T(128)}, s32[128]{0:T(128)S(1)}, u32[]{:S(2)}) copy-start(s32[128]{0:T(128)S(1)} %get-tuple-element.52) | copy-start | bytes 1540
  58.0 218.3 %copy-start.83 = (s32[128]{0:T(128)}, s32[128]{0:T(128)S(1)}, u32[]{:S(2)}) copy-start(s32[128]{0:T(128)S(1)} %get-tuple-element.51) | copy-start | bytes 1540
  61.8 37.2 %all-to-all-start.1 = ((bf16[16,24,2048]{2,1,0:T(8,128)(2,1)}), bf16[16,24,2048]{2,1,0:T(8,128)(2,1)}, u32[]{:S(2)}, u32[]{:S(2)}) async-start(bf16[16,24,2048]{2,1,0:T(8,128)(2,1)} %bitcast.151), calls=%async_computation.1 | async-start | bytes 3145728 | tf_op jit(solution)/shard_map/all_to_all | solution.py:277
  69.3 124.2 %all-gather.12.cloned.1.call-start = ((), (), s32[]{:S(2)}) async-start(), calls=%async_computation.24 | async-start | bytes 11796480 | tf_op jit(solution)/shard_map/all_gather | solution.py:286
  69.4 63.0 %copy-start.108 = (s32[320]{0:T(512)}, s32[320]{0:T(512)S(1)}, u32[]{:S(2)}) copy-start(s32[320]{0:T(512)S(1)} %fusion.164) | copy-start | bytes 3844
  99.0 33.4 %copy-start.120 = (s32[1,3]{1,0:T(1,128)S(1)}, s32[1,3]{1,0:T(1,128)}, u32[]{:S(2)}) copy-start(s32[1,3]{1,0:T(1,128)} %param.21) | copy-start | bytes 40
  99.0 33.6 %copy-start.88 = (s32[1,1024]{1,0:T(1,128)S(1)}, s32[1,1024]{1,0:T(1,128)}, u32[]{:S(2)}) copy-start(s32[1,1024]{1,0:T(1,128)} %param.22) | copy-start | bytes 12292
  99.0 34.4 %slice-start.5 = ((bf16[32,2048]{1,0:T(8,128)(2,1)}), bf16[11,2048]{1,0:T(8,128)(2,1)S(1)}, s32[]{:S(2)}) async-start(bf16[32,2048]{1,0:T(8,128)(2,1)} %copy-done.52), calls=%async_computation.41 | async-start | bytes 131072 | tf_op jit(solution)/shard_map/slice | solution.py:297
  132.6 40.4 %copy-start.81 = (f32[32]{0:T(128)}, f32[32]{0:T(128)S(1)}, u32[]{:S(2)}) copy-start(f32[32]{0:T(128)S(1)} %multiply_power_fusion) | copy-start | bytes 388
  153.1 36.6 %all-to-all-start.2 = ((bf16[16,128,528]{1,2,0:T(8,128)(2,1)}), bf16[16,128,528]{1,2,0:T(8,128)(2,1)}, u32[]{:S(2)}, u32[]{:S(2)}) async-start(bf16[16,128,528]{1,2,0:T(8,128)(2,1)} %broadcast_in_dim.82), calls=%async_computation.2 | async-start | bytes 4325376 | tf_op jit(solution)/shard_map/all_to_all | solution.py:301
  158.4 77.5 %reduce-scatter.8.cloned.1.call-start = ((), (), s32[]{:S(2)}) async-start(), calls=%async_computation.25 | async-start | bytes 4718592 | tf_op jit(solution)/shard_map/reduce_scatter | solution.py:337
  160.7 77.2 %copy-start.61 = (f32[2048]{0:T(1024)}, f32[2048]{0:T(1024)S(1)}, u32[]{:S(2)}) copy-start(f32[2048]{0:T(1024)S(1)} %get-tuple-element.45) | copy-start | bytes 24580
  202.0 71.7 %all-gather.14.cloned.1.call-start = ((), (), s32[]{:S(2)}) async-start(), calls=%async_computation.26 | async-start | bytes 4718592 | tf_op jit(solution)/shard_map/all_gather | solution.py:358
  207.6 28.3 %copy-start.7 = (bf16[128,2048]{1,0:T(8,128)(2,1)S(1)}, bf16[128,2048]{1,0:T(8,128)(2,1)}, u32[]{:S(2)}) copy-start(bf16[128,2048]{1,0:T(8,128)(2,1)} %param.19) | copy-start | bytes 1572868
  240.0 95.0 %all-gather.16.cloned.1.call-start = ((), (), s32[]{:S(2)}) async-start(), calls=%async_computation.27 | async-start | bytes 11796480 | tf_op jit(solution)/shard_map/all_gather | solution.py:360
  241.7 29.8 %copy-start.109 = (s32[320]{0:T(512)S(1)}, s32[320]{0:T(512)}, u32[]{:S(2)}) copy-start(s32[320]{0:T(512)} %copy-done.108) | copy-start | bytes 3844
  277.2 18.1 %all-to-all-start.4 = ((f32[128,1,20]{2,1,0:T(1,128)}), f32[128,1,20]{2,1,0:T(1,128)S(1)}, u32[]{:S(2)}, u32[]{:S(2)}) async-start(f32[128,1,20]{2,1,0:T(1,128)} %bitcast.27), calls=%async_computation.5 | async-start | bytes 131072 | tf_op jit(solution)/shard_map/all_to_all | solution.py:365
  286.4 113.0 %all-gather.18.cloned.1.call-start = ((), (), s32[]{:S(2)}) async-start(), calls=%async_computation.29 | async-start | bytes 4718592 | tf_op jit(solution)/shard_map/all_gather | solution.py:384
  338.2 103.0 %reduce-scatter.10.cloned.1.call-start = ((), (), s32[]{:S(2)}) async-start(), calls=%async_computation.28 | async-start | bytes 11796480 | tf_op jit(solution)/shard_map/reduce_scatter | solution.py:404
  407.4 30.1 %all-to-all-start.6 = ((bf16[16,128,416]{1,2,0:T(8,128)(2,1)}), bf16[16,128,416]{1,2,0:T(8,128)(2,1)}, u32[]{:S(2)}, u32[]{:S(2)}) async-start(bf16[16,128,416]{1,2,0:T(8,128)(2,1)} %copy_bitcast_fusion.1), calls=%async_computation.8 | async-start | bytes 3407872 | tf_op jit(solution)/shard_map/all_to_all | solution.py:167
  411.8 64.4 %reduce-scatter.12.cloned.1.call-start = ((), (), s32[]{:S(2)}) async-start(), calls=%async_computation.30 | async-start | bytes 4718592 | tf_op jit(solution)/shard_map/reduce_scatter | solution.py:441
  447.9 30.9 %copy-start.62 = (f32[2048]{0:T(1024)S(1)}, f32[2048]{0:T(1024)}, u32[]{:S(2)}) copy-start(f32[2048]{0:T(1024)} %copy-done.61) | copy-start | bytes 24580
  447.9 30.9 %copy-start.84 = (s32[128]{0:T(128)S(1)}, s32[128]{0:T(128)}, u32[]{:S(2)}) copy-start(s32[128]{0:T(128)} %copy-done.83) | copy-start | bytes 1540
  447.9 30.9 %copy-start.86 = (s32[128]{0:T(128)S(1)}, s32[128]{0:T(128)}, u32[]{:S(2)}) copy-start(s32[128]{0:T(128)} %copy-done.85) | copy-start | bytes 1540
  447.9 30.9 %copy-start.101 = (f32[128]{0:T(128)S(1)}, f32[128]{0:T(128)}, u32[]{:S(2)}) copy-start(f32[128]{0:T(128)} %copy-done.100) | copy-start | bytes 1540
  447.9 30.8 %all-to-all-start.7 = ((bf16[16,24,2048]{2,1,0:T(8,128)(2,1)}), bf16[16,24,2048]{2,1,0:T(8,128)(2,1)}, u32[]{:S(2)}, u32[]{:S(2)}) async-start(bf16[16,24,2048]{2,1,0:T(8,128)(2,1)} %bitcast.156), calls=%async_computation.10 | async-start | bytes 3145728 | tf_op jit(solution)/shard_map/all_to_all | solution.py:282
  452.4 67.1 %all-gather.20.cloned.1.call-start = ((), (), s32[]{:S(2)}) async-start(), calls=%async_computation.32 | async-start | bytes 4718592 | tf_op jit(solution)/shard_map/all_gather | solution.py:450
  484.3 98.6 %reduce-scatter.14.cloned.1.call-start = ((), (), s32[]{:S(2)}) async-start(), calls=%async_computation.31 | async-start | bytes 11796480 | tf_op jit(solution)/shard_map/reduce_scatter | solution.py:465
  494.8 14.2 %all-to-all-start.8 = ((bf16[8,16,416]{2,1,0:T(8,128)(2,1)}), bf16[8,16,416]{2,1,0:T(8,128)(2,1)S(1)}, u32[]{:S(2)}, u32[]{:S(2)}) async-start(bf16[8,16,416]{2,1,0:T(8,128)(2,1)} %bitcast.38), calls=%async_computation.12 | async-start | bytes 262144 | tf_op jit(solution)/shard_map/all_to_all | solution.py:451
  524.0 25.7 %all-to-all-start.9 = ((bf16[16,16,2048]{2,1,0:T(8,128)(2,1)}), bf16[16,16,2048]{2,1,0:T(8,128)(2,1)}, u32[]{:S(2)}, u32[]{:S(2)}) async-start(bf16[16,16,2048]{2,1,0:T(8,128)(2,1)} %bitcast.161), calls=%async_computation.13 | async-start | bytes 2097152 | tf_op jit(solution)/shard_map/all_to_all | solution.py:167
  531.5 114.6 %reduce-scatter.16.cloned.1.call-start = ((), (), s32[]{:S(2)}) async-start(), calls=%async_computation.33 | async-start | bytes 4718592 | tf_op jit(solution)/shard_map/reduce_scatter | solution.py:512
  592.9 27.0 %all-to-all-start.11 = ((bf16[16,16,2048]{2,1,0:T(8,128)(2,1)}), bf16[16,16,2048]{2,1,0:T(8,128)(2,1)}, u32[]{:S(2)}, u32[]{:S(2)}) async-start(bf16[16,16,2048]{2,1,0:T(8,128)(2,1)} %pad.24), calls=%async_computation.17 | async-start | bytes 2097152 | tf_op jit(solution)/shard_map/all_to_all | solution.py:167
  600.3 127.9 %reduce-scatter.20.cloned.1.call-start = ((), (), s32[]{:S(2)}) async-start(), calls=%async_computation.35 | async-start | bytes 2949120 | tf_op jit(solution)/shard_map/reduce_scatter | solution.py:520
  646.0 108.2 %reduce-scatter.18.cloned.1.call-start = ((), (), s32[]{:S(2)}) async-start(), calls=%async_computation.34 | async-start | bytes 4718592 | tf_op jit(solution)/shard_map/reduce_scatter | solution.py:527
  650.2 28.7 %all-to-all-start.10 = ((bf16[16,24,2048]{2,1,0:T(8,128)(2,1)}), bf16[16,24,2048]{2,1,0:T(8,128)(2,1)}, u32[]{:S(2)}, u32[]{:S(2)}) async-start(bf16[16,24,2048]{2,1,0:T(8,128)(2,1)} %bitcast.155), calls=%async_computation.16 | async-start | bytes 3145728 | tf_op jit(solution)/shard_map/all_to_all | solution.py:282
  678.9 32.5 %all-to-all-start.12 = ((bf16[16,128,512]{2,1,0:T(8,128)(2,1)}), bf16[16,128,512]{2,1,0:T(8,128)(2,1)}, u32[]{:S(2)}, u32[]{:S(2)}) async-start(bf16[16,128,512]{2,1,0:T(8,128)(2,1)} %copy-done.4), calls=%async_computation.18 | async-start | bytes 4194304 | tf_op jit(solution)/shard_map/all_to_all | solution.py:167
  715.3 8.9 %all-to-all-start.13 = ((bf16[8,16,512]{2,1,0:T(8,128)(2,1)}), bf16[8,16,512]{2,1,0:T(8,128)(2,1)S(1)}, u32[]{:S(2)}, u32[]{:S(2)}) async-start(bf16[8,16,512]{2,1,0:T(8,128)(2,1)} %bitcast.46), calls=%async_computation.19 | async-start | bytes 262144 | tf_op jit(solution)/shard_map/all_to_all | solution.py:528
  719.5 30.1 %copy-start.8 = (bf16[128,2048]{1,0:T(8,128)(2,1)S(1)}, bf16[128,2048]{1,0:T(8,128)(2,1)}, u32[]{:S(2)}) copy-start(bf16[128,2048]{1,0:T(8,128)(2,1)} %param.19) | copy-start | bytes 1572868
  719.5 30.1 %copy-start.65 = (f32[2048]{0:T(1024)S(1)}, f32[2048]{0:T(1024)}, u32[]{:S(2)}) copy-start(f32[2048]{0:T(1024)} %copy-done.64) | copy-start | bytes 24580
  721.2 18.8 %collective-permute-start.1 = (bf16[32,2048]{1,0:T(8,128)(2,1)}, bf16[32,2048]{1,0:T(8,128)(2,1)}, u32[]{:S(2)}, u32[]{:S(2)}) collective-permute-start(bf16[32,2048]{1,0:T(8,128)(2,1)} %fusion.56), channel_id=1, source_target_pairs={{0,0},{8,1},{16,2},{24,3},{32,4},{40,5},{48,6},{56,7},{64,8},{72,9... | collective-permute-start | bytes 393224 | tf_op jit(solution)/shard_map/ppermute | solution.py:533
  728.2 17.8 %all-to-all-start.14 = ((bf16[16,16,640]{2,1,0:T(8,128)(2,1)}), bf16[16,16,640]{2,1,0:T(8,128)(2,1)}, u32[]{:S(2)}, u32[]{:S(2)}) async-start(bf16[16,16,640]{2,1,0:T(8,128)(2,1)} %bitcast.169), calls=%async_computation.21 | async-start | bytes 655360 | tf_op jit(solution)/shard_map/all_to_all | solution.py:167
  (112 other events, 638.5 us)
Sparse Core Ops, SparseCore 0:
  9.8 42.2 all-gather.7
  55.9 76.3 all-gather.9
  134.6 57.4 all-gather.11
  202.1 33.7 reduce-scatter.7
  240.1 33.5 all-gather.13
  275.8 59.1 all-gather.15
  338.3 31.7 all-gather.17
  373.2 61.2 reduce-scatter.9
  443.8 32.3 reduce-scatter.11
  484.5 34.9 all-gather.19
  521.9 60.9 reduce-scatter.13
  585.7 36.6 reduce-scatter.15
  646.1 29.4 reduce-scatter.19
  677.8 37.0 reduce-scatter.17

commit v2 on v1

--- a/solution.py
+++ b/solution.py
@@ -463,7 +463,13 @@
         preferred_element_type=F32,
     ).astype(BF)
     expert_own = lax.psum_scatter(expert_part, "shard", scatter_dimension=1, tiled=True)
-    mixed = [in_turn(one, expert_part, ffn_got) for one in mixed]
+    down_sent = jnp.pad(
+        product_tn(in_turn(shared_hidden, attn_grad), cot_group)
+        .astype(BF)
+        .reshape(N_EXPERT, 11, width),
+        ((0, 0), (0, 5), (0, 0)),
+    )
+    mixed = [in_turn(one, expert_part, ffn_got, down_sent) for one in mixed]
 
     attended_grad = product_nt(grad_group, out_w).astype(BF)
     out_sum = sum_over_expert(
@@ -487,14 +493,7 @@
         expanded_grads.append(key_grad[:, :DN])
         expanded_grads.append(value_grad)
         rope_grad = rope_grad + key_grad[:, DN:]
-    down_sum = sum_over_expert(
-        jnp.pad(
-            product_tn(in_turn(shared_hidden, out_sum, rope_grad), cot_group)
-            .astype(BF)
-            .reshape(N_EXPERT, 11, width),
-            ((0, 0), (0, 5), (0, 0)),
-        )
-    )
+    down_sum = sum_over_expert(in_turn(down_sent, out_sum))
     expanded_grad = jnp.concatenate(expanded_grads, axis=1).astype(BF)
     inverse_latent = lax.rsqrt(
         jnp.mean(compressed * compressed, axis=-1, keepdims=True) + EPSILON
@@ -502,6 +501,7 @@
     compressed_grad, _ = rms_backward(
         compressed, inverse_latent, gain_latent, product_nt(expanded_grad, expand_w)
     )
+    compressed_grad = in_turn(compressed_grad, down_sum)
     projected_grad = jnp.concatenate(
         query_grads + [compressed_grad, rotate(rope_grad, cosine, -sine)], axis=1
     ).astype(BF)
@@ -510,11 +510,12 @@
     normed_part = product_nt(projected_grad, query_latent_w).astype(BF)
     expert_own, normed_part = in_order(expert_own, normed_part)
     normed_in_grad = lax.psum_scatter(normed_part, "shard", scatter_dimension=0, tiled=True)
+    expert_back = from_owner(expert_own)
     grads_sent, latent_sent = owner_grads(
         normed_in,
         projected_grad,
         product_tn(latent_normed, expanded_grad).astype(BF).reshape(N_EXPERT, 128, 128),
-        in_turn(ffn_gain, normed_part, down_sum),
+        in_turn(ffn_gain, normed_part, expert_back),
     )
     grads_sum = sum_over_expert(grads_sent)
     latent_own = lax.psum_scatter(
@@ -562,7 +563,6 @@
     )
     grad_input = middle_grad + input_norm_grad
 
-    expert_back = from_owner(expert_own)
     route_out = [product(hot[k].astype(BF), expert_back) for k in range(TOPK)]
     mixture = sum(gate_values[:, k][:, None] * route_out[k] for k in range(TOPK))
     layer_out = (middle + shared_out.astype(F32) + mixture).astype(BF)

time: 774 us -> 758 us (0.979)
  waiting for transfers between devices: 247 us -> 209 us
  other arithmetic: 76 us -> 91.3 us
    all_to_all x5, waiting for transfers between devices: 47.2 us -> 31.4 us  [sum_over_expert(): lax.all_to_all(pieces, 'expert', split_axis=0, concat_axis=0, tiled=True)]
    reduce_max x20 -> x21, other arithmetic: 19.5 us -> 22.1 us  [zero_after(): total = jnp.maximum(total, jnp.max(tile.astype(F32)))]
    unnamed x267 -> x259, local copies, waits for them, and re-layouts: 30.5 us -> 28.6 us
  transfers between devices with their start and end apart: 29 -> 29, of which waited for: 19 -> 15; matrix products, arithmetic and copies ran while one was open for 37% -> 40% of each run, Pallas kernels for 2% -> 2%
where the time goes in v2:
time: 758 us; the launch traced here: 748 us
  waiting for transfers between devices  209 us (28%)
  matrix products  173 us (23%)
  other arithmetic  91.3 us (12%)
  starting transfers between devices  90.5 us (12%)
  local copies, waits for them, and re-layouts  88.5 us (12%)
  blocking collectives  47.5 us (6%)
  between operations  29.9 us (4%)
  Pallas kernels  19.2 us (3%)
    dot_general x15, matrix products, product(): return jnp.dot(left, right, preferred_element_type=F32)  41.4 us
    dot_general x10, matrix products, product_nt(): lax.dot_general(left, right, (((1,), (1,)), ((), ())), preferred_element_...  36.9 us
    all_to_all x5, waiting for transfers between devices, sum_over_expert(): lax.all_to_all(pieces, 'expert', split_axis=0, concat_axis=0, tiled=True)  31.4 us
    dot_general x13, matrix products, product_tn(): lax.dot_general(left, right, (((0,), (0,)), ((), ())), preferred_element_...  30.9 us
    all_gather x1, waiting for transfers between devices, body(): lax.all_gather(in_turn(jnp.concatenate([columns[:, :1280], turned[:16].re...  29.8 us
    all_to_all x1, waiting for transfers between devices, to_owner(): lax.all_to_all(packed, 'expert', split_axis=0, concat_axis=0, tiled=True)  29.7 us
    all_to_all x1, blocking collectives, to_owner(): lax.all_to_all(packed, 'expert', split_axis=0, concat_axis=0, tiled=True)  29.5 us
    all_to_all x5, starting transfers between devices, sum_over_expert(): lax.all_to_all(pieces, 'expert', split_axis=0, concat_axis=0, tiled=True)  28.6 us
  transfers between devices with their start and end apart: 29, of which 15 were waited for; matrix products, arithmetic and copies ran while one was open for 40% of the time, Pallas kernels for 2%

profile of v2, /device:TPU:8, one launch (start us, length us, event | category | flops | bytes accessed | tf_op | source)
XLA Modules:
  0.0 748.4 jit_solution(17183195892248853693)
XLA Ops:
  15.6 5.0 all-to-all-start
  20.8 5.3 collective-permute-start
  26.1 11.9 %collective-permute-done = bf16[32,2048]{1,0:T(8,128)(2,1)S(1)} collective-permute-done((bf16[32,2048]{1,0:T(8,128)(2,1)S(1)}, bf16[32,2048]{1,0:T(8,128)(2,1)S(1)}, u32[]{:S(2)}, u32[]{:S(2)}) %collective-permute-start) | collective-permute-done | bytes 131104 | tf_op jit(solution)/shard_map/ppermute | solution.py:233
  40.4 11.6 %all-gather.8.cloned.1.call-done = bf16[1024,2048]{1,0:T(8,128)(2,1)} async-done(((bf16[128,2048]{1,0:T(8,128)(2,1)}), bf16[1024,2048]{1,0:T(8,128)(2,1)}) %all-gather.8.cloned.1.call-update) | async-done | bytes 4194320 | tf_op jit(solution)/shard_map/all_gather | solution.py:215
  61.8 7.5 %all-to-all-start.1 = ((bf16[16,24,2048]{2,1,0:T(8,128)(2,1)}), bf16[16,24,2048]{2,1,0:T(8,128)(2,1)}, u32[]{:S(2)}, u32[]{:S(2)}) async-start(bf16[16,24,2048]{2,1,0:T(8,128)(2,1)} %bitcast.151), calls=%async_computation.1 | async-start | bytes 3145728 | tf_op jit(solution)/shard_map/all_to_all | solution.py:277
  69.4 29.7 %all-to-all-done.1 = bf16[16,24,2048]{2,1,0:T(8,128)(2,1)} async-done(((bf16[16,24,2048]{2,1,0:T(8,128)(2,1)}), bf16[16,24,2048]{2,1,0:T(8,128)(2,1)}, u32[]{:S(2)}, u32[]{:S(2)}) %all-to-all-start.1) | async-done | bytes 1572896 | tf_op jit(solution)/shard_map/all_to_all | solution.py:277
  102.5 29.8 %all-gather.10.cloned.1.call-done = bf16[2048,1536]{1,0:T(8,128)(2,1)} async-done(((bf16[128,1536]{1,0:T(8,128)(2,1)}), bf16[2048,1536]{1,0:T(8,128)(2,1)}) %all-gather.10.cloned.1.call-update) | async-done | bytes 6291472 | tf_op jit(solution)/shard_map/all_gather | solution.py:238
  153.0 5.3 all-to-all-start.2
  163.9 8.1 %fusion.190 = (bf16[1024,960]{0,1:T(8,128)(2,1)S(1)}, f32[1024,960]{0,1:T(8,128)S(1)}) fusion(bf16[1024,2048]{1,0:T(8,128)(2,1)S(1)} %fusion.2.normed_ref, bf16[2048,1536]{1,0:T(8,128)(2,1)} %all-gather.10.cloned.1.call-done), kind=kOutput, calls=%fused_computation.378 | convolution fusion | flops 4027514880 | bytes 14286848 | tf_op jit(solution)/shard_map/dot_general | solution.py:33
  186.0 3.6 all-to-all-done.2
  197.4 4.5 convolution_convert_fusion.4
  210.9 25.0 %reduce-scatter.8.cloned.1.call-done = bf16[128,2048]{1,0:T(8,128)(2,1)} async-done(((bf16[1024,2048]{1,0:T(8,128)(2,1)}), bf16[128,2048]{1,0:T(8,128)(2,1)}) %reduce-scatter.8.cloned.1.call-update) | async-done | bytes 524304 | tf_op jit(solution)/shard_map/reduce_scatter | solution.py:337
  241.7 29.5 %all_to_all.121 = bf16[16,24,2048]{2,1,0:T(8,128)(2,1)S(1)} all-to-all(bf16[16,24,2048]{2,1,0:T(8,128)(2,1)S(1)} %bitcast.152), channel_id=1, replica_groups=mesh['expert'=16,'shard'=8] {'expert'}, dimensions={0} | all-to-all | bytes 3145728 | tf_op jit(solution)/shard_map/all_to_all | solution.py:277
  277.1 9.1 %all-to-all-start.4 = ((f32[128,1,20]{2,1,0:T(1,128)}), f32[128,1,20]{2,1,0:T(1,128)S(1)}, u32[]{:S(2)}, u32[]{:S(2)}) async-start(f32[128,1,20]{2,1,0:T(1,128)} %bitcast.27), calls=%async_computation.5 | async-start | bytes 131072 | tf_op jit(solution)/shard_map/all_to_all | solution.py:365
  290.8 4.6 reshape.496
  300.7 4.4 fusion.7
  312.5 22.3 %all-gather.16.cloned.1.call-done = bf16[4,640,2048]{2,1,0:T(8,128)(2,1)} async-done(((bf16[4,80,2048]{2,1,0:T(8,128)(2,1)}), bf16[4,640,2048]{2,1,0:T(8,128)(2,1)}) %all-gather.16.cloned.1.call-update) | async-done | bytes 10485776 | tf_op jit(solution)/shard_map/all_gather | solution.py:360
  339.5 12.1 %fusion.195 = f32[4,640,352]{1,2,0:T(8,128)} fusion(bf16[4,640,2048]{2,1,0:T(8,128)(2,1)} %all-gather.16.cloned.1.call-done, bf16[4,352,2048]{2,1,0:T(8,128)(2,1)} %copy-done.13), kind=kOutput, calls=%fused_computation.383 | convolution fusion | flops 3690987520 | bytes 19857408 | tf_op jit(solution)/shard_map/jsd,jfd->jsf/dot_general | solution.py:386
  351.6 10.7 %fusion.20 = (f32[4,640]{1,0:T(4,128)S(1)}, bf16[4,640,176]{1,2,0:T(8,128)(2,1)}, bf16[4,640,176]{1,2,0:T(8,128)(2,1)}, bf16[4,640,176]{1,2,0:T(8,128)(2,1)}) fusion(f32[4,640]{1,0:T(4,128)S(1)} %mul.555, bf16[]{:T(256)S(6)} %select_n.171, f32[4,640,352]{1,2,0:T(8,128)} %fusion.195, bf16[4,640,2048]{2,1,0:T(8,128)(2,1)} %all-gather.12.cloned.1.call-done, ...), kind=kOutput, calls=%fused_computation.63 | convolution fusion | flops 1854502400 | bytes 19697666 | tf_op jit(solution)/shard_map/jsd,jfd->jsf/dot_general | solution.py:392
  362.2 10.7 %convolution_convert_fusion.1 = bf16[4,640,2048]{2,1,0:T(8,128)(2,1)} fusion(bf16[4,352,2048]{2,1,0:T(8,128)(2,1)} %copy-done.13, bf16[4,640,176]{1,2,0:T(8,128)(2,1)} %get-tuple-element.62, bf16[4,640,176]{1,2,0:T(8,128)(2,1)} %get-tuple-element.61), kind=kOutput, calls=%fused_computation.6 | convolution fusion | flops 3699834880 | bytes 18055168 | tf_op jit(solution)/shard_map/jsf,jfd->jsd/dot_general | solution.py:398
  377.1 18.0 %all_to_all.122 = f32[128,1,20]{2,1,0:T(1,128)S(1)} all-to-all(f32[128,1,20]{2,1,0:T(1,128)S(1)} %copy.230), channel_id=1, replica_groups=mesh['expert'=16,'shard'=8] {'expert','shard'}, dimensions={0} | all-to-all | bytes 20480 | tf_op jit(solution)/shard_map/all_to_all | solution.py:410
  399.5 4.8 multiply_convert_fusion.8
  407.5 4.4 all-to-all-start.6
  413.2 6.1 convolution_convert_fusion.2
  419.3 18.2 %all-to-all-done.6 = bf16[16,128,416]{1,2,0:T(8,128)(2,1)} async-done(((bf16[16,128,416]{1,2,0:T(8,128)(2,1)}), bf16[16,128,416]{1,2,0:T(8,128)(2,1)}, u32[]{:S(2)}, u32[]{:S(2)}) %all-to-all-start.6) | async-done | bytes 1703968 | tf_op jit(solution)/shard_map/all_to_all | solution.py:167
  444.3 3.6 convolution_convert_fusion.7
  447.9 4.6 all-to-all-start.7
  452.5 23.8 %reduce-scatter.12.cloned.1.call-done = bf16[128,2048]{1,0:T(8,128)(2,1)} async-done(((bf16[1024,2048]{1,0:T(8,128)(2,1)}), bf16[128,2048]{1,0:T(8,128)(2,1)}) %reduce-scatter.12.cloned.1.call-update) | async-done | bytes 524304 | tf_op jit(solution)/shard_map/reduce_scatter | solution.py:441
  486.6 6.7 convolution_convert_fusion
  496.5 8.4 %all-to-all-start.8 = ((bf16[8,16,416]{2,1,0:T(8,128)(2,1)}), bf16[8,16,416]{2,1,0:T(8,128)(2,1)}, u32[]{:S(2)}, u32[]{:S(2)}) async-start(bf16[8,16,416]{2,1,0:T(8,128)(2,1)} %bitcast.38), calls=%async_computation.12 | async-start | bytes 262144 | tf_op jit(solution)/shard_map/all_to_all | solution.py:451
  504.9 4.1 convolution_convert_fusion.13
  515.2 4.5 all-gather.20.cloned.1.call-done
  519.7 4.5 convolution_convert_fusion.12
  524.2 7.0 all-to-all-start.9
  531.2 4.6 convolution_convert_fusion.17
  539.2 10.3 %all-to-all-done.9 = bf16[16,16,2048]{2,1,0:T(8,128)(2,1)} async-done(((bf16[16,16,2048]{2,1,0:T(8,128)(2,1)}), bf16[16,16,2048]{2,1,0:T(8,128)(2,1)}, u32[]{:S(2)}, u32[]{:S(2)}) %all-to-all-start.9) | async-done | bytes 1048608 | tf_op jit(solution)/shard_map/all_to_all | solution.py:167
  555.8 4.3 all-to-all-start.10
  583.9 3.7 fusion.33
  590.0 9.6 %convolution_convert_fusion.5 = bf16[1024,2048]{1,0:T(8,128)(2,1)} fusion(bf16[1024,960]{0,1:T(8,128)(2,1)} %fusion.142, bf16[2048,1536]{1,0:T(8,128)(2,1)} %all-gather.10.cloned.1.call-done), kind=kOutput, calls=%fused_computation.20 | convolution fusion | flops 4028628992 | bytes 10354688 | tf_op jit(solution)/shard_map/dot_general | solution.py:41
  603.8 7.3 all-to-all-start.11
  619.1 13.0 %all-to-all-done.11 = bf16[16,24,2048]{2,1,0:T(8,128)(2,1)} async-done(((bf16[16,24,2048]{2,1,0:T(8,128)(2,1)}), bf16[16,24,2048]{2,1,0:T(8,128)(2,1)}, u32[]{:S(2)}, u32[]{:S(2)}) %all-to-all-start.11) | async-done | bytes 1572896 | tf_op jit(solution)/shard_map/all_to_all | solution.py:282
  637.8 15.2 %shard_map.309 = (bf16[16,128,512]{2,1,0:T(8,128)(2,1)S(1)}, bf16[8,256,640]{2,1,0:T(8,128)(2,1)S(1)}) custom-call(bf16[1024,2048]{1,0:T(8,128)(2,1)S(1)} %copy-done.2, bf16[960,1024]{1,0:T(8,128)(2,1)} %bitcast.45.grad_ref, bf16[16,128,128]{2,1,0:T(8,128)(2,1)S(1)} %reshape.507.expand_ref, f32[16,128,128]{2,1,0:T(8,128)S(1)} %pad_add_fusion.gain_ref), custom_call_target="tpu_custom_call" | custom-call | flops 4026531840 | bytes 12582912 | tf_op jit(solution)/shard_map/pallas_call | solution.py:138
  660.6 4.6 all-to-all-start.12
  670.2 9.2 %fusion.40 = f32[4,176,2048]{2,1,0:T(8,128)} fusion(bf16[4,640,2048]{2,1,0:T(8,128)(2,1)} %all-gather.16.cloned.1.call-done, bf16[4,640,176]{1,2,0:T(8,128)(2,1)S(1)} %copy-done.38, bf16[]{:T(256)S(6)} %select_n.181), kind=kOutput, calls=%fused_computation.107 | convolution fusion | flops 1845944320 | bytes 17154050 | tf_op jit(solution)/shard_map/jsf,jsd->jfd/dot_general | solution.py:546
  679.4 9.2 %fusion.38 = f32[4,176,2048]{2,1,0:T(8,128)} fusion(bf16[4,640,2048]{2,1,0:T(8,128)(2,1)} %all-gather.16.cloned.1.call-done, bf16[4,640,176]{1,2,0:T(8,128)(2,1)S(1)} %copy-done.37, bf16[]{:T(256)S(6)} %select_n.181), kind=kOutput, calls=%fused_computation.105 | convolution fusion | flops 1845944320 | bytes 17154050 | tf_op jit(solution)/shard_map/jsf,jsd->jfd/dot_general | solution.py:552
  688.6 5.0 fusion.36
  697.4 5.0 all-to-all-start.13
  712.0 8.3 %all-to-all-start.14 = ((bf16[16,16,640]{2,1,0:T(8,128)(2,1)}), bf16[16,16,640]{2,1,0:T(8,128)(2,1)}, u32[]{:S(2)}, u32[]{:S(2)}) async-start(bf16[16,16,640]{2,1,0:T(8,128)(2,1)} %bitcast.167), calls=%async_computation.21 | async-start | bytes 655360 | tf_op jit(solution)/shard_map/all_to_all | solution.py:167
  (512 shorter events, 240.0 us)
Async XLA Ops:
  7.2 344.4 %copy-start = (bf16[4,176,2048]{2,1,0:T(8,128)(2,1)S(1)}, bf16[4,176,2048]{2,1,0:T(8,128)(2,1)}, u32[]{:S(2)}) copy-start(bf16[4,176,2048]{2,1,0:T(8,128)(2,1)} %param.37) | copy-start | bytes 8650756
  7.2 44.8 %all-gather.8.cloned.1.call-start = ((), (), s32[]{:S(2)}) async-start(), calls=%async_computation.22 | async-start | bytes 4718592 | tf_op jit(solution)/shard_map/all_gather | solution.py:215
  14.6 41.1 %copy-start.92 = (s32[128,2]{0,1:T(2,128)S(1)}, s32[128,2]{0,1:T(2,128)}, u32[]{:S(2)}) copy-start(s32[128,2]{0,1:T(2,128)} %param.23) | copy-start | bytes 3076
  15.5 44.4 %copy-start.16 = (bf16[128,2048]{1,0:T(8,128)(2,1)S(1)}, bf16[128,2048]{1,0:T(8,128)(2,1)}, u32[]{:S(2)}) copy-start(bf16[128,2048]{1,0:T(8,128)(2,1)} %param.20) | copy-start | bytes 1572868
  15.6 23.1 %all-to-all-start = ((bf16[8,16,1632]{2,1,0:T(8,128)(2,1)}), bf16[8,16,1632]{2,1,0:T(8,128)(2,1)}, u32[]{:S(2)}, u32[]{:S(2)}) async-start(bf16[8,16,1632]{2,1,0:T(8,128)(2,1)} %concatenate.73), calls=%async_computation | async-start | bytes 851968 | tf_op jit(solution)/shard_map/all_to_all | solution.py:232
  20.6 111.6 %all-gather.10.cloned.1.call-start = ((), (), s32[]{:S(2)}) async-start(), calls=%async_computation.23 | async-start | bytes 6684672 | tf_op jit(solution)/shard_map/all_gather | solution.py:238
  20.8 17.2 %collective-permute-start = (bf16[32,2048]{1,0:T(8,128)(2,1)S(1)}, bf16[32,2048]{1,0:T(8,128)(2,1)S(1)}, u32[]{:S(2)}, u32[]{:S(2)}) collective-permute-start(bf16[32,2048]{1,0:T(8,128)(2,1)S(1)} %maximum_maximum_fusion), channel_id=1, source_target_pairs={{0,0},{1,8},{2,16},{3,24},{4,32},{5,40},{6,48},{7,56},{8,64},{9,72... | collective-permute-start | bytes 393224 | tf_op jit(solution)/shard_map/ppermute | solution.py:233
  58.0 217.8 %copy-start.82 = (s32[128]{0:T(128)}, s32[128]{0:T(128)S(1)}, u32[]{:S(2)}) copy-start(s32[128]{0:T(128)S(1)} %get-tuple-element.52) | copy-start | bytes 1540
  58.0 218.3 %copy-start.79 = (s32[128]{0:T(128)}, s32[128]{0:T(128)S(1)}, u32[]{:S(2)}) copy-start(s32[128]{0:T(128)S(1)} %get-tuple-element.51) | copy-start | bytes 1540
  61.8 37.3 %all-to-all-start.1 = ((bf16[16,24,2048]{2,1,0:T(8,128)(2,1)}), bf16[16,24,2048]{2,1,0:T(8,128)(2,1)}, u32[]{:S(2)}, u32[]{:S(2)}) async-start(bf16[16,24,2048]{2,1,0:T(8,128)(2,1)} %bitcast.151), calls=%async_computation.1 | async-start | bytes 3145728 | tf_op jit(solution)/shard_map/all_to_all | solution.py:277
  69.3 124.2 %all-gather.12.cloned.1.call-start = ((), (), s32[]{:S(2)}) async-start(), calls=%async_computation.24 | async-start | bytes 11796480 | tf_op jit(solution)/shard_map/all_gather | solution.py:286
  69.4 62.9 %copy-start.106 = (s32[320]{0:T(512)}, s32[320]{0:T(512)S(1)}, u32[]{:S(2)}) copy-start(s32[320]{0:T(512)S(1)} %fusion.164) | copy-start | bytes 3844
  99.1 33.2 %copy-start.118 = (s32[1,3]{1,0:T(1,128)S(1)}, s32[1,3]{1,0:T(1,128)}, u32[]{:S(2)}) copy-start(s32[1,3]{1,0:T(1,128)} %param.21) | copy-start | bytes 40
  99.1 33.4 %copy-start.85 = (s32[1,1024]{1,0:T(1,128)S(1)}, s32[1,1024]{1,0:T(1,128)}, u32[]{:S(2)}) copy-start(s32[1,1024]{1,0:T(1,128)} %param.22) | copy-start | bytes 12292
  99.1 34.2 %slice-start.3 = ((bf16[32,2048]{1,0:T(8,128)(2,1)}), bf16[11,2048]{1,0:T(8,128)(2,1)S(1)}, s32[]{:S(2)}) async-start(bf16[32,2048]{1,0:T(8,128)(2,1)} %copy-done.46), calls=%async_computation.39 | async-start | bytes 131072 | tf_op jit(solution)/shard_map/slice | solution.py:297
  132.5 40.4 %copy-start.76 = (f32[32]{0:T(128)}, f32[32]{0:T(128)S(1)}, u32[]{:S(2)}) copy-start(f32[32]{0:T(128)S(1)} %multiply_power_fusion) | copy-start | bytes 388
  153.0 36.6 %all-to-all-start.2 = ((bf16[16,128,528]{1,2,0:T(8,128)(2,1)}), bf16[16,128,528]{1,2,0:T(8,128)(2,1)}, u32[]{:S(2)}, u32[]{:S(2)}) async-start(bf16[16,128,528]{1,2,0:T(8,128)(2,1)} %broadcast_in_dim.82), calls=%async_computation.2 | async-start | bytes 4325376 | tf_op jit(solution)/shard_map/all_to_all | solution.py:301
  158.4 77.5 %reduce-scatter.8.cloned.1.call-start = ((), (), s32[]{:S(2)}) async-start(), calls=%async_computation.25 | async-start | bytes 4718592 | tf_op jit(solution)/shard_map/reduce_scatter | solution.py:337
  160.6 77.2 %copy-start.55 = (f32[2048]{0:T(1024)}, f32[2048]{0:T(1024)S(1)}, u32[]{:S(2)}) copy-start(f32[2048]{0:T(1024)S(1)} %get-tuple-element.45) | copy-start | bytes 24580
  201.9 71.6 %all-gather.14.cloned.1.call-start = ((), (), s32[]{:S(2)}) async-start(), calls=%async_computation.26 | async-start | bytes 4718592 | tf_op jit(solution)/shard_map/all_gather | solution.py:358
  207.6 28.3 %copy-start.5 = (bf16[128,2048]{1,0:T(8,128)(2,1)S(1)}, bf16[128,2048]{1,0:T(8,128)(2,1)}, u32[]{:S(2)}) copy-start(bf16[128,2048]{1,0:T(8,128)(2,1)} %param.19) | copy-start | bytes 1572868
  239.9 95.0 %all-gather.16.cloned.1.call-start = ((), (), s32[]{:S(2)}) async-start(), calls=%async_computation.27 | async-start | bytes 11796480 | tf_op jit(solution)/shard_map/all_gather | solution.py:360
  241.7 29.5 %copy-start.107 = (s32[320]{0:T(512)S(1)}, s32[320]{0:T(512)}, u32[]{:S(2)}) copy-start(s32[320]{0:T(512)} %copy-done.106) | copy-start | bytes 3844
  277.1 18.2 %all-to-all-start.4 = ((f32[128,1,20]{2,1,0:T(1,128)}), f32[128,1,20]{2,1,0:T(1,128)S(1)}, u32[]{:S(2)}, u32[]{:S(2)}) async-start(f32[128,1,20]{2,1,0:T(1,128)} %bitcast.27), calls=%async_computation.5 | async-start | bytes 131072 | tf_op jit(solution)/shard_map/all_to_all | solution.py:365
  286.3 113.2 %all-gather.18.cloned.1.call-start = ((), (), s32[]{:S(2)}) async-start(), calls=%async_computation.29 | async-start | bytes 4718592 | tf_op jit(solution)/shard_map/all_gather | solution.py:384
  338.1 103.1 %reduce-scatter.10.cloned.1.call-start = ((), (), s32[]{:S(2)}) async-start(), calls=%async_computation.28 | async-start | bytes 11796480 | tf_op jit(solution)/shard_map/reduce_scatter | solution.py:404
  407.5 30.0 %all-to-all-start.6 = ((bf16[16,128,416]{1,2,0:T(8,128)(2,1)}), bf16[16,128,416]{1,2,0:T(8,128)(2,1)}, u32[]{:S(2)}, u32[]{:S(2)}) async-start(bf16[16,128,416]{1,2,0:T(8,128)(2,1)} %copy_bitcast_fusion.1), calls=%async_computation.8 | async-start | bytes 3407872 | tf_op jit(solution)/shard_map/all_to_all | solution.py:167
  411.9 64.4 %reduce-scatter.12.cloned.1.call-start = ((), (), s32[]{:S(2)}) async-start(), calls=%async_computation.30 | async-start | bytes 4718592 | tf_op jit(solution)/shard_map/reduce_scatter | solution.py:441
  447.9 30.9 %copy-start.56 = (f32[2048]{0:T(1024)S(1)}, f32[2048]{0:T(1024)}, u32[]{:S(2)}) copy-start(f32[2048]{0:T(1024)} %copy-done.55) | copy-start | bytes 24580
  447.9 30.9 %copy-start.80 = (s32[128]{0:T(128)S(1)}, s32[128]{0:T(128)}, u32[]{:S(2)}) copy-start(s32[128]{0:T(128)} %copy-done.79) | copy-start | bytes 1540
  447.9 30.9 %copy-start.83 = (s32[128]{0:T(128)S(1)}, s32[128]{0:T(128)}, u32[]{:S(2)}) copy-start(s32[128]{0:T(128)} %copy-done.82) | copy-start | bytes 1540
  447.9 30.9 %copy-start.99 = (f32[128]{0:T(128)S(1)}, f32[128]{0:T(128)}, u32[]{:S(2)}) copy-start(f32[128]{0:T(128)} %copy-done.98) | copy-start | bytes 1540
  447.9 30.9 %all-to-all-start.7 = ((bf16[16,24,2048]{2,1,0:T(8,128)(2,1)}), bf16[16,24,2048]{2,1,0:T(8,128)(2,1)}, u32[]{:S(2)}, u32[]{:S(2)}) async-start(bf16[16,24,2048]{2,1,0:T(8,128)(2,1)} %bitcast.154), calls=%async_computation.10 | async-start | bytes 3145728 | tf_op jit(solution)/shard_map/all_to_all | solution.py:282
  452.5 67.2 %all-gather.20.cloned.1.call-start = ((), (), s32[]{:S(2)}) async-start(), calls=%async_computation.32 | async-start | bytes 4718592 | tf_op jit(solution)/shard_map/all_gather | solution.py:450
  484.6 115.1 %reduce-scatter.14.cloned.1.call-start = ((), (), s32[]{:S(2)}) async-start(), calls=%async_computation.31 | async-start | bytes 11796480 | tf_op jit(solution)/shard_map/reduce_scatter | solution.py:465
  496.5 16.8 %all-to-all-start.8 = ((bf16[8,16,416]{2,1,0:T(8,128)(2,1)}), bf16[8,16,416]{2,1,0:T(8,128)(2,1)}, u32[]{:S(2)}, u32[]{:S(2)}) async-start(bf16[8,16,416]{2,1,0:T(8,128)(2,1)} %bitcast.38), calls=%async_computation.12 | async-start | bytes 262144 | tf_op jit(solution)/shard_map/all_to_all | solution.py:451
  524.2 25.3 %all-to-all-start.9 = ((bf16[16,16,2048]{2,1,0:T(8,128)(2,1)}), bf16[16,16,2048]{2,1,0:T(8,128)(2,1)}, u32[]{:S(2)}, u32[]{:S(2)}) async-start(bf16[16,16,2048]{2,1,0:T(8,128)(2,1)} %bitcast.160), calls=%async_computation.13 | async-start | bytes 2097152 | tf_op jit(solution)/shard_map/all_to_all | solution.py:167
  555.8 24.8 %all-to-all-start.10 = ((bf16[16,16,2048]{2,1,0:T(8,128)(2,1)}), bf16[16,16,2048]{2,1,0:T(8,128)(2,1)}, u32[]{:S(2)}, u32[]{:S(2)}) async-start(bf16[16,16,2048]{2,1,0:T(8,128)(2,1)} %get-tuple-element.73), calls=%async_computation.14 | async-start | bytes 2097152 | tf_op jit(solution)/shard_map/all_to_all | solution.py:167
  560.1 95.9 %reduce-scatter.16.cloned.1.call-start = ((), (), s32[]{:S(2)}) async-start(), calls=%async_computation.33 | async-start | bytes 4718592 | tf_op jit(solution)/shard_map/reduce_scatter | solution.py:512
  603.8 28.3 %all-to-all-start.11 = ((bf16[16,24,2048]{2,1,0:T(8,128)(2,1)}), bf16[16,24,2048]{2,1,0:T(8,128)(2,1)}, u32[]{:S(2)}, u32[]{:S(2)}) async-start(bf16[16,24,2048]{2,1,0:T(8,128)(2,1)} %bitcast.153), calls=%async_computation.17 | async-start | bytes 3145728 | tf_op jit(solution)/shard_map/all_to_all | solution.py:282
  611.1 100.9 %reduce-scatter.20.cloned.1.call-start = ((), (), s32[]{:S(2)}) async-start(), calls=%async_computation.35 | async-start | bytes 2949120 | tf_op jit(solution)/shard_map/reduce_scatter | solution.py:521
  656.0 82.2 %reduce-scatter.18.cloned.1.call-start = ((), (), s32[]{:S(2)}) async-start(), calls=%async_computation.34 | async-start | bytes 4718592 | tf_op jit(solution)/shard_map/reduce_scatter | solution.py:528
  660.6 32.9 %all-to-all-start.12 = ((bf16[16,128,512]{2,1,0:T(8,128)(2,1)}), bf16[16,128,512]{2,1,0:T(8,128)(2,1)}, u32[]{:S(2)}, u32[]{:S(2)}) async-start(bf16[16,128,512]{2,1,0:T(8,128)(2,1)} %copy-done.4), calls=%async_computation.18 | async-start | bytes 4194304 | tf_op jit(solution)/shard_map/all_to_all | solution.py:167
  697.4 10.6 %all-to-all-start.13 = ((bf16[8,16,512]{2,1,0:T(8,128)(2,1)}), bf16[8,16,512]{2,1,0:T(8,128)(2,1)S(1)}, u32[]{:S(2)}, u32[]{:S(2)}) async-start(bf16[8,16,512]{2,1,0:T(8,128)(2,1)} %bitcast.47), calls=%async_computation.19 | async-start | bytes 262144 | tf_op jit(solution)/shard_map/all_to_all | solution.py:529
  702.4 31.3 %copy-start.6 = (bf16[128,2048]{1,0:T(8,128)(2,1)S(1)}, bf16[128,2048]{1,0:T(8,128)(2,1)}, u32[]{:S(2)}) copy-start(bf16[128,2048]{1,0:T(8,128)(2,1)} %param.19) | copy-start | bytes 1572868
  702.4 31.3 %copy-start.59 = (f32[2048]{0:T(1024)S(1)}, f32[2048]{0:T(1024)}, u32[]{:S(2)}) copy-start(f32[2048]{0:T(1024)} %copy-done.58) | copy-start | bytes 24580
  704.1 20.0 %collective-permute-start.1 = (bf16[32,2048]{1,0:T(8,128)(2,1)}, bf16[32,2048]{1,0:T(8,128)(2,1)}, u32[]{:S(2)}, u32[]{:S(2)}) collective-permute-start(bf16[32,2048]{1,0:T(8,128)(2,1)} %fusion.56), channel_id=1, source_target_pairs={{0,0},{8,1},{16,2},{24,3},{32,4},{40,5},{48,6},{56,7},{64,8},{72,9... | collective-permute-start | bytes 393224 | tf_op jit(solution)/shard_map/ppermute | solution.py:534
  712.0 18.0 %all-to-all-start.14 = ((bf16[16,16,640]{2,1,0:T(8,128)(2,1)}), bf16[16,16,640]{2,1,0:T(8,128)(2,1)}, u32[]{:S(2)}, u32[]{:S(2)}) async-start(bf16[16,16,640]{2,1,0:T(8,128)(2,1)} %bitcast.167), calls=%async_computation.21 | async-start | bytes 655360 | tf_op jit(solution)/shard_map/all_to_all | solution.py:167
  (108 other events, 593.3 us)
Sparse Core Ops, SparseCore 0:
  9.8 42.2 all-gather.7
  55.8 76.3 all-gather.9
  134.5 57.4 all-gather.11
  202.1 33.7 reduce-scatter.7
  240.0 33.5 all-gather.13
  275.7 59.1 all-gather.15
  338.2 31.7 all-gather.17
  373.1 61.2 reduce-scatter.9
  443.8 32.4 reduce-scatter.11
  484.7 34.9 all-gather.19
  522.1 60.9 reduce-scatter.13
  599.8 35.9 reduce-scatter.15
  656.1 29.7 reduce-scatter.19
  688.2 41.9 reduce-scatter.17
